TPU v7x, 32 devices: a whole 2x2x4 slice. The times are simulated.
32 devices in a mesh: rows: 16 (over z, y, core), blk: 2 (over x).
Axes of the slice: x: 2, y: 2, z: 4, core: 2. Of those that a mesh axis runs over, the one named last changes fastest.
Arguments:
- hidden: bfloat16 [16, 768, 1280], P('rows', 'blk'), may hold values from -6 to 6
- starts: int32 [16, 4], P('rows'), may hold values from 0 to 767, as said below
- first_gain: float32 [1280], replicated, may hold values from 0.5 to 2
- first_shift: float32 [1280], replicated, may hold values from -3 to 3
- qkv_weight: bfloat16 [1280, 3840], P('rows'), may hold values from -0.15625 to 0.15625
- out_weight: bfloat16 [1280, 1280], P('rows'), may hold values from -0.625 to 0.625
- second_gain: float32 [1280], replicated, may hold values from 0.5 to 2
- second_shift: float32 [1280], replicated, may hold values from -3 to 3
- up_weight: bfloat16 [1280, 5120], P('rows'), may hold values from -0.15625 to 0.15625
- hidden_bias: float32 [5120], replicated, may hold values from -3 to 3
- down_weight: bfloat16 [5120, 1280], P('rows'), may hold values from -0.078125 to 0.078125
- cotangent: bfloat16 [16, 768, 1280], P('rows', 'blk'), may hold values from -6 to 6
Outputs:
- output: float32 [16, 768, 1280], P('rows', 'blk')
- grad_hidden: float32 [16, 768, 1280], P('rows', 'blk')
- grad_qkv: float32 [1280, 3840], P('rows')
- grad_out: float32 [1280, 1280], P('rows')
- grad_up: float32 [1280, 5120], P('rows')
- grad_down: float32 [5120, 1280], P('rows')
- grad_first_gain: float32 [1280], replicated
- grad_first_shift: float32 [1280], replicated
- grad_second_gain: float32 [1280], replicated
- grad_second_shift: float32 [1280], replicated
- grad_hidden_bias: float32 [5120], replicated
Inputs may be any that keep to these rules, and one draw needn't show every extreme that they name: Each row of starts lists the first positions (CLS tokens) of its 4 cells in increasing order, beginning with 0; every cell holds one position or more, and a cell runs up to the next start (the last up to 768). In every row one cell begins among the first 384 positions and ends among the last 384.
All inputs are finite; a program needn't handle non-finite values.
Results may differ from a plain program's by a relative error of at most 0.02.
Values may be sent and summed in bfloat16 or wider, within the bound.
A program may use at most 256 MiB of HBM per device.

v0:
```python
import math

import jax
import jax.numpy as jnp
from jax import lax
from jax.sharding import PartitionSpec as P

HEADS = 20
HEAD_DIM = 64


masked_score = -1e30
block_limit = 512


def layer_norm(values, gain, shift):
    mean_value = jnp.mean(values, axis=-1, keepdims=True)
    centred = values - mean_value
    variance = jnp.mean(centred * centred, axis=-1, keepdims=True)
    return centred * lax.rsqrt(variance + 1e-05) * gain + shift


def segment_of(starts_row, positions):
    reached = starts_row[None, :] <= positions[:, None]
    return jnp.sum(reached.astype(jnp.int32), axis=1) - 1


def scores_with_mask(queries, key_block, query_seg, key_seg):
    products = jnp.einsum("qhe,khe->hqk", queries, key_block, preferred_element_type=jnp.float32)
    products = products * queries.shape[2] ** (-0.5)
    allowed = (query_seg[:, None] == key_seg[None, :])[None, :, :]
    return (jnp.where(allowed, products, masked_score), allowed)


def attend_rows(running, key_rows, value_rows, queries, query_seg, starts_row):
    piece_rows = key_rows.shape[0]
    step_rows = math.gcd(piece_rows, block_limit)
    head_count = queries.shape[1]
    head_width = queries.shape[2]

    def one_block(block_index, state):
        row_top, denominator, weighted = state
        block_start = block_index * step_rows
        key_block = lax.dynamic_slice_in_dim(key_rows, block_start, step_rows, 0).reshape(
            step_rows, head_count, head_width
        )
        value_block = lax.dynamic_slice_in_dim(value_rows, block_start, step_rows, 0).reshape(
            step_rows, head_count, head_width
        )
        key_seg = segment_of(starts_row, block_start + jnp.arange(step_rows, dtype=jnp.int32))
        scores, allowed = scores_with_mask(queries, key_block, query_seg, key_seg)
        new_top = jnp.maximum(row_top, jnp.max(scores, axis=-1))
        factor = jnp.exp(row_top - new_top)
        weights = jnp.where(allowed, jnp.exp(scores - new_top[:, :, None]), 0.0)
        denominator = denominator * factor + jnp.sum(weights, axis=-1)
        weighted = weighted * factor[:, :, None] + jnp.einsum(
            "hqk,khe->hqe",
            weights.astype(jnp.bfloat16),
            value_block,
            preferred_element_type=jnp.float32,
        )
        return (new_top, denominator, weighted)

    return lax.fori_loop(0, piece_rows // step_rows, one_block, running)


def on_device(
    hidden,
    starts,
    first_gain,
    first_shift,
    qkv_weight,
    out_weight,
    second_gain,
    second_shift,
    up_weight,
    hidden_bias,
    down_weight,
    cotangent,
):
    rows_here = hidden.shape[1]
    model_width = hidden.shape[2]
    head_count = HEADS
    head_width = HEAD_DIM
    score_scale = head_width ** (-0.5)
    inputs = hidden[0].astype(jnp.float32)
    starts_row = starts[0]
    offset = lax.axis_index("blk") * rows_here
    query_seg = segment_of(starts_row, offset + jnp.arange(rows_here, dtype=jnp.int32))
    qkv_full, out_full, up_full, down_full = (
        lax.all_gather(qkv_weight, "rows", axis=0, tiled=True),
        lax.all_gather(out_weight, "rows", axis=0, tiled=True),
        lax.all_gather(up_weight, "rows", axis=0, tiled=True),
        lax.all_gather(down_weight, "rows", axis=0, tiled=True),
    )
    normed_low = layer_norm(inputs, first_gain, first_shift).astype(jnp.bfloat16)
    packed = jnp.dot(normed_low, qkv_full, preferred_element_type=jnp.float32).astype(jnp.bfloat16)
    queries = packed[:, :model_width].reshape(rows_here, head_count, head_width)
    key_rows = packed[:, model_width : 2 * model_width]
    value_rows = packed[:, 2 * model_width :]
    initial = (
        jnp.full((head_count, rows_here), masked_score, jnp.float32),
        jnp.zeros((head_count, rows_here), jnp.float32),
        jnp.zeros((head_count, rows_here, head_width), jnp.float32),
    )
    row_top, denominator, weighted = attend_rows(
        initial,
        lax.all_gather(key_rows, "blk", axis=0, tiled=True),
        lax.all_gather(value_rows, "blk", axis=0, tiled=True),
        queries,
        query_seg,
        starts_row,
    )
    log_total = row_top + jnp.log(denominator)
    attended = jnp.transpose(weighted / denominator[:, :, None], (1, 0, 2))
    attended_low = attended.reshape(rows_here, model_width).astype(jnp.bfloat16)
    residual = inputs + jnp.dot(attended_low, out_full, preferred_element_type=jnp.float32)
    second_low = layer_norm(residual, second_gain, second_shift).astype(jnp.bfloat16)
    up_values = jnp.dot(second_low, up_full, preferred_element_type=jnp.float32) + hidden_bias
    activated_low = jax.nn.gelu(up_values, approximate=False).astype(jnp.bfloat16)
    output = residual + jnp.dot(activated_low, down_full, preferred_element_type=jnp.float32)
    cot_low = cotangent[0]
    d_activated = jnp.einsum("tc,fc->tf", cot_low, down_full, preferred_element_type=jnp.float32)
    unused_gelu, gelu_pull = jax.vjp(
        lambda values: jax.nn.gelu(values, approximate=False), up_values
    )
    d_up_low = gelu_pull(d_activated)[0].astype(jnp.bfloat16)
    d_second = jnp.einsum("tf,cf->tc", d_up_low, up_full, preferred_element_type=jnp.float32)
    unused_second, second_pull = jax.vjp(layer_norm, residual, second_gain, second_shift)
    d_norm_two, d_second_gain, d_second_shift = second_pull(d_second)
    d_residual = cot_low.astype(jnp.float32) + d_norm_two
    d_branch_low = d_residual.astype(jnp.bfloat16)
    d_attended_low = jnp.einsum(
        "tc,kc->tk", d_branch_low, out_full, preferred_element_type=jnp.float32
    ).astype(jnp.bfloat16)
    d_attended3 = d_attended_low.reshape(rows_here, head_count, head_width)
    row_dots = jnp.einsum("qhe,qhe->hq", d_attended3.astype(jnp.float32), attended)
    keys_all, values_all = (
        lax.all_gather(key_rows, "blk", axis=0, tiled=True),
        lax.all_gather(value_rows, "blk", axis=0, tiled=True),
    )
    length = keys_all.shape[0]
    step_rows = math.gcd(length, block_limit)

    def block_terms(block_index):
        block_start = block_index * step_rows
        key_block = lax.dynamic_slice_in_dim(keys_all, block_start, step_rows, 0).reshape(
            step_rows, head_count, head_width
        )
        value_block = lax.dynamic_slice_in_dim(values_all, block_start, step_rows, 0).reshape(
            step_rows, head_count, head_width
        )
        key_seg = segment_of(starts_row, block_start + jnp.arange(step_rows, dtype=jnp.int32))
        scores, allowed = scores_with_mask(queries, key_block, query_seg, key_seg)
        probability = jnp.where(allowed, jnp.exp(scores - log_total[:, :, None]), 0.0)
        d_probs = jnp.einsum(
            "qhe,khe->hqk", d_attended3, value_block, preferred_element_type=jnp.float32
        )
        d_scores = (probability * (d_probs - row_dots[:, :, None])).astype(jnp.bfloat16)
        return (key_block, probability, d_scores)

    dq_start = jnp.zeros((rows_here, head_count, head_width), jnp.float32)

    def back_block(dq_sum, block_index):
        key_block, probability, d_scores = block_terms(block_index)
        dq_sum = dq_sum + jnp.einsum(
            "hqk,khe->qhe", d_scores, key_block, preferred_element_type=jnp.float32
        )
        dk_block = (
            jnp.einsum("hqk,qhe->khe", d_scores, queries, preferred_element_type=jnp.float32)
            * score_scale
        )
        dv_block = jnp.einsum(
            "hqk,qhe->khe",
            probability.astype(jnp.bfloat16),
            d_attended3,
            preferred_element_type=jnp.float32,
        )
        return (
            dq_sum,
            (dk_block.reshape(step_rows, model_width), dv_block.reshape(step_rows, model_width)),
        )

    dq_sum, (dk_terms, dv_terms) = lax.scan(back_block, dq_start, jnp.arange(length // step_rows))
    dk_rows, dv_rows = (
        lax.psum_scatter(
            dk_terms.reshape(length, model_width).astype(jnp.bfloat16),
            "blk",
            scatter_dimension=0,
            tiled=True,
        ).astype(jnp.float32),
        lax.psum_scatter(
            dv_terms.reshape(length, model_width).astype(jnp.bfloat16),
            "blk",
            scatter_dimension=0,
            tiled=True,
        ).astype(jnp.float32),
    )
    d_packed = jnp.concatenate(
        [(dq_sum * score_scale).reshape(rows_here, model_width), dk_rows, dv_rows], axis=1
    ).astype(jnp.bfloat16)
    d_normed = jnp.einsum("tn,cn->tc", d_packed, qkv_full, preferred_element_type=jnp.float32)
    unused_first, first_pull = jax.vjp(layer_norm, inputs, first_gain, first_shift)
    d_norm_one, d_first_gain, d_first_shift = first_pull(d_normed)
    grad_hidden = d_residual + d_norm_one
    d_bias = jnp.sum(d_up_low, axis=0, dtype=jnp.float32)
    wide_share = lax.psum_scatter(
        jnp.concatenate(
            [
                jnp.einsum("tc,tn->cn", normed_low, d_packed, preferred_element_type=jnp.float32),
                jnp.einsum(
                    "tc,tn->cn", attended_low, d_branch_low, preferred_element_type=jnp.float32
                ),
                jnp.einsum("tc,tn->cn", second_low, d_up_low, preferred_element_type=jnp.float32),
            ],
            axis=1,
        ).astype(jnp.bfloat16),
        "rows",
        scatter_dimension=0,
        tiled=True,
    )
    down_share = lax.psum_scatter(
        jnp.einsum("tf,tn->fn", activated_low, cot_low, preferred_element_type=jnp.float32).astype(
            jnp.bfloat16
        ),
        "rows",
        scatter_dimension=0,
        tiled=True,
    )
    wide_grads, down_grads = (
        lax.psum(wide_share, "blk").astype(jnp.float32),
        lax.psum(down_share, "blk").astype(jnp.float32),
    )
    grad_qkv = wide_grads[:, : 3 * model_width]
    grad_out = wide_grads[:, 3 * model_width : 4 * model_width]
    grad_up = wide_grads[:, 4 * model_width :]
    small_grads = lax.psum(
        (d_first_gain, d_first_shift, d_second_gain, d_second_shift, d_bias), ("rows", "blk")
    )
    return (
        output[None],
        grad_hidden[None],
        grad_qkv,
        grad_out,
        grad_up,
        down_grads,
        small_grads[0],
        small_grads[1],
        small_grads[2],
        small_grads[3],
        small_grads[4],
    )


def solution(mesh):
    in_specs = (
        P("rows", "blk", None),
        P("rows", None),
        P(),
        P(),
        P("rows", None),
        P("rows", None),
        P(),
        P(),
        P("rows", None),
        P(),
        P("rows", None),
        P("rows", "blk", None),
    )
    out_specs = (
        P("rows", "blk", None),
        P("rows", "blk", None),
        P("rows", None),
        P("rows", None),
        P("rows", None),
        P("rows", None),
        P(),
        P(),
        P(),
        P(),
        P(),
    )
    return jax.shard_map(
        on_device, mesh=mesh, in_specs=in_specs, out_specs=out_specs, check_vma=False
    )
```

profile of v0, /device:TPU:0, one launch (start us, length us, event | category | flops | bytes accessed | tf_op | source)
XLA Modules:
  0.0 1083.6 jit_solution(2859159625004029418)
XLA Ops:
  11.6 85.3 %all-gather.7.cloned.1.call-done = bf16[1280,3840]{1,0:T(8,128)(2,1)} async-done(((bf16[80,3840]{1,0:T(8,128)(2,1)}), bf16[1280,3840]{1,0:T(8,128)(2,1)}) %all-gather.7.cloned.1.call-update) | async-done | bytes 9830416 | tf_op jit(solution)/shard_map/all_gather | solution.py:91
  96.9 8.3 convolution_convert_fusion.4
  110.6 26.1 %all-gather.9.cloned.1.call-done = bf16[768,1280]{1,0:T(8,128)(2,1)} async-done(((bf16[384,1280]{1,0:T(8,128)(2,1)}), bf16[768,1280]{1,0:T(8,128)(2,1)}) %all-gather.9.cloned.1.call-update) | async-done | bytes 1966096 | tf_op jit(solution)/shard_map/all_gather | solution.py:108
  140.7 29.8 %all-gather.11.cloned.1.call-done = bf16[768,1280]{1,0:T(8,128)(2,1)} async-done(((bf16[384,1280]{1,0:T(8,128)(2,1)}), bf16[768,1280]{1,0:T(8,128)(2,1)}) %all-gather.11.cloned.1.call-update) | async-done | bytes 1966096 | tf_op jit(solution)/shard_map/all_gather | solution.py:109
  174.5 49.5 %while.37 = (s32[]{:T(128)}, f32[20,384]{1,0:T(8,128)S(1)}, f32[20,384]{1,0:T(8,128)S(1)}, f32[20,384,64]{1,2,0:T(8,128)}, s32[384]{0:T(512)S(1)}, /*index=5*/s3...) while((s32[]{:T(128)}, f32[20,384]{1,0:T(8,128)S(1)}, ...), condition=%wide.region_7.8_spmd.clone, body=%wide.region_3.7_spmd.clone.sunk | while | flops 530490112 | bytes 64790256 | solution.py:64
  195.9 5.7 fusion.118
  232.7 90.8 %all-gather.15.cloned.1.call-done = bf16[1280,5120]{1,0:T(8,128)(2,1)} async-done(((bf16[80,5120]{1,0:T(8,128)(2,1)}), bf16[1280,5120]{1,0:T(8,128)(2,1)}) %all-gather.15.cloned.1.call-update) | async-done | bytes 13107216 | tf_op jit(solution)/shard_map/all_gather | solution.py:93
  323.5 26.7 %multiply_convert_fusion = (bf16[384,5120]{1,0:T(8,128)(2,1)}, f32[384,5120]{1,0:T(8,128)}, f32[384,5120]{1,0:T(8,128)}) fusion(f32[5120]{0:T(1024)S(1)} %copy-done.38, bf16[1280,5120]{1,0:T(8,128)(2,1)} %all-gather.15.cloned.1.call-done, f32[384,1280]{1,0:T(8,128)} %copy-done.8, f32[1280]{0:T(1024)S(1)} %copy-done.39, f32[1280]{0:T(1024)S(1)} %copy-done.34, ...), kind=kOutput, calls=%fused_computation.52 | convolution fusion | flops 5165383680 | bytes 34767872 | tf_op jit(solution)/shard_map/dot_general | solution.py:119
  350.2 77.6 %all-gather.17.cloned.1.call-done = bf16[5120,1280]{1,0:T(8,128)(2,1)} async-done(((bf16[320,1280]{1,0:T(8,128)(2,1)}), bf16[5120,1280]{1,0:T(8,128)(2,1)}) %all-gather.17.cloned.1.call-update) | async-done | bytes 13107216 | tf_op jit(solution)/shard_map/all_gather | solution.py:94
  427.8 16.1 %convert_reduce_fusion.2 = (f32[5120]{0:T(1024)}, bf16[384,5120]{1,0:T(8,128)(2,1)}) fusion(f32[384,5120]{1,0:T(8,128)} %get-tuple-element.647, f32[384,5120]{1,0:T(8,128)} %get-tuple-element.659, bf16[5120,1280]{1,0:T(8,128)(2,1)} %all-gather.17.cloned.1.call-done, bf16[1,384,1280]{2,1,0:T(8,128)(2,1)} %param.27), kind=kOutput, calls=%fused_computation.50 | convolution fusion | flops 5064616960 | bytes 33771520 | tf_op jit(solution)/shard_map/tc,fc->tf/dot_general | solution.py:123
  443.9 11.7 %multiply_reduce_fusion = (f32[1280]{0:T(1024)}, f32[384]{0:T(512)S(1)}, f32[1280]{0:T(1024)}, f32[384,1280]{1,0:T(8,128)S(1)}) fusion(f32[384,1280]{1,0:T(8,128)S(1)} %copy-done.9, f32[384]{0:T(512)S(1)} %fusion.52, f32[384]{0:T(512)S(1)} %broadcast_multiply_fusion, f32[1280]{0:T(1024)S(1)} %copy-done.34, bf16[384,5120]{1,0:T(8,128)(2,1)} %get-tuple-element.663, ...), kind=kOutput, calls=%fused_computation.93 | convolution fusion | flops 5037093888 | bytes 20991488 | tf_op jit(solution)/shard_map/tf,cf->tc/dot_general | solution.py:128
  465.1 71.5 %while.38 = (s32[]{:T(128)}, f32[384,20,64]{0,2,1:T(8,128)}, bf16[3,256,1280]{2,1,0:T(8,128)(2,1)}, bf16[3,256,1280]{2,1,0:T(8,128)(2,1)}, s32[3]{0:T(128)S(1)},...) while((s32[]{:T(128)}, f32[384,20,64]{0,2,1:T(8,128)}, ...), condition=%wide.region_14.15_spmd.clone, body=%wide.region_12.0_spmd.clone.sunk | while | flops 1283624192 | bytes 121636704 | solution.py:184
  537.7 13.1 %convolution_convert_fusion = bf16[5120,1280]{1,0:T(8,128)(2,1)} fusion(bf16[384,5120]{1,0:T(8,128)(2,1)} %get-tuple-element.646, bf16[1,384,1280]{2,1,0:T(8,128)(2,1)S(1)} %copy-done.15), kind=kOutput, calls=%fused_computation.45 | convolution fusion | flops 5039718400 | bytes 18022400 | tf_op jit(solution)/shard_map/tf,tn->fn/dot_general | solution.py:223
  556.0 6.3 copy.93
  562.5 13.1 %convolution_convert_fusion.1 = bf16[1280,5120]{1,0:T(8,128)(2,1)} fusion(bf16[384,5120]{1,0:T(8,128)(2,1)} %get-tuple-element.663, f32[384,1280]{1,0:T(8,128)} %copy-done.8, f32[1280]{0:T(1024)S(1)} %copy-done.40, f32[1280]{0:T(1024)S(1)} %copy-done.34, f32[384]{0:T(512)S(1)} %fusion.52, f32[384]{0:T(512)S(1)} %broadcast_multiply_fusion), kind=kOutput, calls=%fused_computation.46 | convolution fusion | flops 5042176000 | bytes 19018752 | tf_op jit(solution)/shard_map/tc,tn->cn/dot_general | solution.py:214
  577.3 20.7 %reduce-scatter.13.cloned.1.call-done = bf16[384,1280]{1,0:T(8,128)(2,1)} async-done(((bf16[768,1280]{1,0:T(8,128)(2,1)}), bf16[384,1280]{1,0:T(8,128)(2,1)}) %reduce-scatter.13.cloned.1.call-update) | async-done | bytes 983056
  600.3 9.4 convolution_convert_fusion.2
  609.7 21.7 %pad_maximum_fusion = bf16[1280,10240]{1,0:T(8,128)(2,1)} fusion(bf16[1280,5120]{1,0:T(8,128)(2,1)} %convolution_convert_fusion.1, bf16[1280,1280]{1,0:T(8,128)(2,1)} %copy.93, bf16[1280,3840]{1,0:T(8,128)(2,1)} %convolution_convert_fusion.2), kind=kLoop, calls=%fused_computation.44 | loop fusion | flops 78643200 | bytes 52428800 | tf_op jit(solution)/shard_map/concatenate | solution.py:208
  632.9 13.0 %fusion.30 = f32[1,384,1280]{2,1,0:T(8,128)} fusion(f32[384,1280]{1,0:T(8,128)S(1)} %copy-done.10, bf16[384,5120]{1,0:T(8,128)(2,1)} %get-tuple-element.646, bf16[5120,1280]{1,0:T(8,128)(2,1)} %all-gather.17.cloned.1.call-done), kind=kOutput, calls=%fused_computation.71 | convolution fusion | flops 5033656320 | bytes 20971520 | tf_op jit(solution)/shard_map/dot_general | solution.py:121
  645.9 94.6 %reduce-scatter.11.cloned.1.call-done = bf16[320,1280]{1,0:T(8,128)(2,1)} async-done(((bf16[5120,1280]{1,0:T(8,128)(2,1)}), bf16[320,1280]{1,0:T(8,128)(2,1)}) %reduce-scatter.11.cloned.1.call-update) | async-done | bytes 819216 | tf_op jit(solution)/shard_map/reduce_scatter | solution.py:222
  740.5 255.9 %reduce-scatter.9.cloned.1.call-done = bf16[80,10240]{1,0:T(8,128)(2,1)} async-done(((bf16[1280,10240]{1,0:T(8,128)(2,1)}), bf16[80,10240]{1,0:T(8,128)(2,1)}) %reduce-scatter.9.cloned.1.call-update) | async-done | bytes 1638416 | tf_op jit(solution)/shard_map/reduce_scatter | solution.py:207
  996.6 9.0 fusion.58
  1007.8 41.2 %all-reduce = (f32[1280]{0:T(1024)}, f32[1280]{0:T(1024)}, f32[1280]{0:T(1024)}, f32[1280]{0:T(1024)}, f32[5120]{0:T(1024)}) all-reduce(f32[1280]{0:T(1024)S(1)} %get-tuple-element.586, f32[1280]{0:T(1024)S(1)} %get-tuple-element.589, f32[1280]{0:T(1024)S(1)} %copy-done.35, ...), channel_id=1, replica_groups=mesh['rows'=16,'blk'=2] {'rows','blk'}, use_global_device_ids=true, to_apply=%region_24.25 | all-reduce | flops 10240 | bytes 81920 | tf_op jit(solution)/shard_map/psum | solution.py:237
  1052.9 17.4 %all-reduce.4.cloned.1.call-done = (bf16[80,10240]{1,0:T(8,128)(2,1)}, bf16[320,1280]{1,0:T(8,128)(2,1)}) async-done(((bf16[80,10240]{1,0:T(8,128)(2,1)}, bf16[320,1280]{1,0:T(8,128)(2,1)}), (bf16[80,10240]{1,0:T(8,128)(2,1)}, bf16[320,1280]{1,0:T(8,128)(2,1)})) %all-reduce.4.cloned.1.call-update) | async-done | bytes 2457616 | tf_op jit(solution)/shard_map/psum | solution.py:231
  (244 shorter events, 173.3 us)
Async XLA Ops:
  7.2 89.7 %all-gather.7.cloned.1.call-start = ((), (), s32[]{:S(2)}) async-start(), calls=%async_computation.4 | async-start | bytes 10444800 | tf_op jit(solution)/shard_map/all_gather | solution.py:91
  7.9 128.8 %all-gather.9.cloned.1.call-start = ((), (), s32[]{:S(2)}) async-start(), calls=%async_computation.5 | async-start | bytes 2949120 | tf_op jit(solution)/shard_map/all_gather | solution.py:108
  9.4 95.8 %copy-start.24 = (f32[384]{0:T(512)}, f32[384]{0:T(512)S(1)}, u32[]{:S(2)}) copy-start(f32[384]{0:T(512)S(1)} %broadcast_multiply_fusion.1) | copy-start | bytes 4612
  11.6 93.6 %copy-start.32 = (f32[384]{0:T(512)}, f32[384]{0:T(512)S(1)}, u32[]{:S(2)}) copy-start(f32[384]{0:T(512)S(1)} %fusion.51) | copy-start | bytes 4612
  106.7 63.8 %all-gather.11.cloned.1.call-start = ((), (), s32[]{:S(2)}) async-start(), calls=%async_computation.6 | async-start | bytes 2949120 | tf_op jit(solution)/shard_map/all_gather | solution.py:109
  107.5 119.3 %all-gather.13.cloned.1.call-start = ((), (), s32[]{:S(2)}) async-start(), calls=%async_computation.7 | async-start | bytes 3481600 | tf_op jit(solution)/shard_map/all_gather | solution.py:92
  108.0 215.5 %all-gather.15.cloned.1.call-start = ((), (), s32[]{:S(2)}) async-start(), calls=%async_computation.8 | async-start | bytes 13926400 | tf_op jit(solution)/shard_map/all_gather | solution.py:93
  108.6 319.2 %all-gather.17.cloned.1.call-start = ((), (), s32[]{:S(2)}) async-start(), calls=%async_computation.9 | async-start | bytes 13926400 | tf_op jit(solution)/shard_map/all_gather | solution.py:94
  109.2 466.4 %reduce-scatter.15.cloned.1.call-start = ((), (), s32[]{:S(2)}) async-start(), calls=%async_computation.13 | async-start | bytes 2949120
  174.5 52.2 %copy-start.6 = (bf16[1,384,1280]{2,1,0:T(8,128)(2,1)S(1)}, bf16[1,384,1280]{2,1,0:T(8,128)(2,1)}, u32[]{:S(2)}) copy-start(bf16[1,384,1280]{2,1,0:T(8,128)(2,1)} %param.16) | copy-start | bytes 2949124
  226.8 96.8 %copy-start.34 = (f32[1280]{0:T(1024)S(1)}, f32[1280]{0:T(1024)}, u32[]{:S(2)}) copy-start(f32[1280]{0:T(1024)} %param.22) | copy-start | bytes 15364
  226.8 96.8 %copy-start.38 = (f32[5120]{0:T(1024)S(1)}, f32[5120]{0:T(1024)}, u32[]{:S(2)}) copy-start(f32[5120]{0:T(1024)} %param.25) | copy-start | bytes 61444
  226.8 96.7 %copy-start.39 = (f32[1280]{0:T(1024)S(1)}, f32[1280]{0:T(1024)}, u32[]{:S(2)}) copy-start(f32[1280]{0:T(1024)} %param.23) | copy-start | bytes 15364
  536.6 61.4 %reduce-scatter.13.cloned.1.call-start = ((), (), s32[]{:S(2)}) async-start(), calls=%async_computation.12 | async-start | bytes 2949120
  537.3 203.2 %reduce-scatter.11.cloned.1.call-start = ((), (), s32[]{:S(2)}) async-start(), calls=%async_computation.11 | async-start | bytes 13926400 | tf_op jit(solution)/shard_map/reduce_scatter | solution.py:222
  550.9 445.6 %reduce-scatter.9.cloned.1.call-start = ((), (), s32[]{:S(2)}) async-start(), calls=%async_computation.10 | async-start | bytes 27852800 | tf_op jit(solution)/shard_map/reduce_scatter | solution.py:207
  562.5 37.8 %copy-start.20 = (bf16[384,20,64]{0,2,1:T(8,128)(2,1)}, bf16[384,20,64]{0,2,1:T(8,128)(2,1)S(1)}, u32[]{:S(2)}) copy-start(bf16[384,20,64]{0,2,1:T(8,128)(2,1)S(1)} %multiply_convert_fusion.1) | copy-start | bytes 2949124
  575.5 24.7 %copy-start.26 = (f32[1280]{0:T(1024)S(1)}, f32[1280]{0:T(1024)}, u32[]{:S(2)}) copy-start(f32[1280]{0:T(1024)} %param.18) | copy-start | bytes 15364
  575.6 24.7 %copy-start.33 = (f32[384]{0:T(512)S(1)}, f32[384]{0:T(512)}, u32[]{:S(2)}) copy-start(f32[384]{0:T(512)} %copy-done.32) | copy-start | bytes 4612
  575.6 24.7 %copy-start.41 = (f32[1280]{0:T(1024)S(1)}, f32[1280]{0:T(1024)}, u32[]{:S(2)}) copy-start(f32[1280]{0:T(1024)} %param.19) | copy-start | bytes 15364
  577.3 32.4 %copy-start.21 = (bf16[384,1280]{0,1:T(8,128)(2,1)}, bf16[384,1280]{0,1:T(8,128)(2,1)S(1)}, u32[]{:S(2)}) copy-start(bf16[384,1280]{0,1:T(8,128)(2,1)S(1)} %copy.109) | copy-start | bytes 2949124
  631.4 438.9 %all-reduce.4.cloned.1.call-start = ((), (), s32[]{:S(2)}) async-start(), calls=%async_computation.14 | async-start | bytes 4915200 | tf_op jit(solution)/shard_map/psum | solution.py:231
  996.6 52.4 %copy-start.29 = (f32[384]{0:T(512)S(1)}, f32[384]{0:T(512)}, u32[]{:S(2)}) copy-start(f32[384]{0:T(512)} %copy-done.28) | copy-start | bytes 4612
  1005.6 43.3 %copy-start.5 = (f32[384,1280]{1,0:T(8,128)S(1)}, f32[384,1280]{1,0:T(8,128)}, u32[]{:S(2)}) copy-start(f32[384,1280]{1,0:T(8,128)} %copy-done.4) | copy-start | bytes 5898244
  (37 other events, 216.4 us)
Sparse Core Ops, SparseCore 0:
  10.3 86.5 all-gather.6
  106.8 29.8 all-gather.8
  138.9 31.5 all-gather.10
  172.6 45.7 all-gather.12
  220.6 102.8 all-gather.14
  325.6 102.1 all-gather.16
  536.7 28.4 reduce-scatter.14
  567.6 30.3 reduce-scatter.12
  602.1 138.3 reduce-scatter.10
  745.2 251.2 reduce-scatter.8
  999.0 71.2 all-reduce.3
where the time goes:
time: 1090 us; the launch traced here: 1080 us
  waiting for transfers between devices  702 us (64%)
  matrix products  206 us (19%)
  local copies, waits for them, and re-layouts  62.1 us (6%)
  other arithmetic  54.4 us (5%)
  blocking collectives  41.2 us (4%)
  between operations  14.5 us (1%)
    reduce_scatter x1, waiting for transfers between devices, on_device(): lax.psum_scatter(jnp.concatenate([jnp.einsum('tc,tn->cn', normed_low, d_p...  256 us
    reduce_scatter x1, waiting for transfers between devices, on_device(): lax.psum_scatter(jnp.einsum('tf,tn->fn', activated_low, cot_low, preferre...  94.6 us
    all_gather x1, waiting for transfers between devices, on_device(): lax.all_gather(up_weight, 'rows', axis=0, tiled=True)  90.8 us
    all_gather x1, waiting for transfers between devices, on_device(): lax.all_gather(qkv_weight, 'rows', axis=0, tiled=True)  85.3 us
    all_gather x1, waiting for transfers between devices, on_device(): lax.all_gather(down_weight, 'rows', axis=0, tiled=True)  77.6 us
    psum x1, blocking collectives, on_device(): lax.psum((d_first_gain, d_first_shift, d_second_gain, d_second_shift, d_b...  41.2 us
    all_gather x1, waiting for transfers between devices, on_device(): lax.all_gather(value_rows, 'blk', axis=0, tiled=True)  29.8 us
    dot_general x1, matrix products, on_device(): jnp.dot(second_low, up_full, preferred_element_type=jnp.float32)  26.7 us
  transfers between devices with their start and end apart: 11, of which 9 were waited for; matrix products, arithmetic and copies ran while one was open for 18% of the time, Pallas kernels for 0%

commit v1 on v0

--- a/solution.py
+++ b/solution.py
@@ -252,6 +252,131 @@
     )
 
 
+def split_layer(
+    hidden, starts, first_gain, first_shift, qkv_weight, out_weight, second_gain, second_shift,
+    up_weight, hidden_bias, down_weight, cotangent,
+):
+    own_rows, width = hidden.shape[1], hidden.shape[2]
+    pieces = lax.axis_size("blk")
+    piece = lax.axis_index("blk")
+    shards = lax.axis_size("rows")
+    heads = HEADS // pieces
+    cols = heads * HEAD_DIM
+    length = own_rows * pieces
+    units = down_weight.shape[0] // pieces
+    scale = HEAD_DIM ** (-0.5)
+    starts_row = starts[0]
+
+    qkv_own = lax.dynamic_index_in_dim(
+        qkv_weight.reshape(-1, 3, pieces, cols), piece, 2, keepdims=False
+    ).reshape(-1, 3 * cols)
+    up_own = lax.dynamic_index_in_dim(
+        up_weight.reshape(-1, shards, pieces, units), piece, 2, keepdims=False
+    ).reshape(-1, shards * units)
+    bias_own = lax.dynamic_index_in_dim(
+        hidden_bias.reshape(shards, pieces, units), piece, 1, keepdims=False
+    ).reshape(-1)
+    down_own = lax.dynamic_slice_in_dim(down_weight, piece * units, units, 0)
+    hidden_all = lax.all_gather(hidden[0], "blk", axis=0, tiled=True)
+    dy_all = lax.all_gather(cotangent[0], "blk", axis=0, tiled=True)
+    qkv_all = lax.all_gather(qkv_own, "rows", axis=0, tiled=True)
+    out_all = lax.all_gather(out_weight, "rows", axis=0, tiled=True)
+    up_all = lax.all_gather(up_own, "rows", axis=0, tiled=True)
+    down_all = lax.all_gather(down_own, "rows", axis=0, tiled=True)
+
+    f32 = jnp.float32
+    bf16 = jnp.bfloat16
+    normed = layer_norm(hidden_all.astype(f32), first_gain, first_shift).astype(bf16)
+    packed = jnp.dot(normed, qkv_all, preferred_element_type=f32).astype(bf16)
+    q, k, v = (
+        packed[:, i * cols : (i + 1) * cols].reshape(length, heads, HEAD_DIM).transpose(1, 0, 2)
+        for i in range(3)
+    )
+    seg = segment_of(starts_row, jnp.arange(length, dtype=jnp.int32))
+    allowed = (seg[:, None] == seg[None, :])[None]
+    scores = jnp.einsum("hqe,hke->hqk", q, k, preferred_element_type=f32) * scale
+    scores = jnp.where(allowed, scores, masked_score)
+    top = jnp.max(scores, axis=-1, keepdims=True)
+    weights = jnp.exp(scores - top)
+    total = jnp.sum(weights, axis=-1, keepdims=True)
+    log_total = top + jnp.log(total)
+    attended = jnp.einsum(
+        "hqk,hke->hqe", (weights / total).astype(bf16), v, preferred_element_type=f32
+    )
+    attended_part = attended.transpose(1, 0, 2).reshape(length, cols).astype(bf16)
+    attended_low = lax.all_to_all(attended_part, "blk", 0, 1, tiled=True)
+    inputs = hidden[0].astype(f32)
+    residual = inputs + jnp.dot(attended_low, out_all, preferred_element_type=f32)
+    second_own = layer_norm(residual, second_gain, second_shift).astype(bf16)
+    second = lax.all_gather(second_own, "blk", axis=0, tiled=True)
+    up_values = jnp.dot(second, up_all, preferred_element_type=f32) + bias_own
+    activated = jax.nn.gelu(up_values, approximate=False).astype(bf16)
+    down_part = jnp.dot(activated, down_all, preferred_element_type=f32).astype(bf16)
+    output = residual + lax.psum_scatter(
+        down_part, "blk", scatter_dimension=0, tiled=True
+    ).astype(f32)
+
+    grad_down = jnp.einsum("tf,tn->fn", activated, dy_all, preferred_element_type=f32)
+    d_act = jnp.einsum("tc,fc->tf", dy_all, down_all, preferred_element_type=f32)
+    _, gelu_pull = jax.vjp(lambda u: jax.nn.gelu(u, approximate=False), up_values)
+    d_up = gelu_pull(d_act)[0].astype(bf16)
+    grad_up = jnp.einsum("tc,tn->cn", second, d_up, preferred_element_type=f32)
+    d_second_part = jnp.einsum("tf,cf->tc", d_up, up_all, preferred_element_type=f32)
+    d_second = lax.psum_scatter(
+        d_second_part.astype(bf16), "blk", scatter_dimension=0, tiled=True
+    ).astype(f32)
+    _, second_pull = jax.vjp(layer_norm, residual, second_gain, second_shift)
+    d_norm_two, d_second_gain, d_second_shift = second_pull(d_second)
+    d_residual = cotangent[0].astype(f32) + d_norm_two
+    d_branch = d_residual.astype(bf16)
+    grad_out = jnp.einsum("tc,tn->cn", attended_low, d_branch, preferred_element_type=f32)
+    d_att_own = jnp.einsum("tc,kc->tk", d_branch, out_all, preferred_element_type=f32)
+    d_att = lax.all_to_all(d_att_own.astype(bf16), "blk", 1, 0, tiled=True)
+    d_att3 = d_att.reshape(length, heads, HEAD_DIM).transpose(1, 0, 2)
+    row_dots = jnp.sum(d_att3.astype(f32) * attended, axis=-1, keepdims=True)
+    probs = jnp.where(allowed, jnp.exp(scores - log_total), 0.0)
+    d_probs = jnp.einsum("hqe,hke->hqk", d_att3, v, preferred_element_type=f32)
+    d_scores = (probs * (d_probs - row_dots)).astype(bf16)
+    dq = jnp.einsum("hqk,hke->qhe", d_scores, k, preferred_element_type=f32) * scale
+    dk = jnp.einsum("hqk,hqe->khe", d_scores, q, preferred_element_type=f32) * scale
+    dv = jnp.einsum("hqk,hqe->khe", probs.astype(bf16), d_att3, preferred_element_type=f32)
+    d_packed = jnp.concatenate([t.reshape(length, cols) for t in (dq, dk, dv)], axis=1).astype(bf16)
+    grad_qkv = jnp.einsum("tc,tn->cn", normed, d_packed, preferred_element_type=f32)
+    d_normed_part = jnp.einsum("tn,cn->tc", d_packed, qkv_all, preferred_element_type=f32)
+    d_normed = lax.psum_scatter(
+        d_normed_part.astype(bf16), "blk", scatter_dimension=0, tiled=True
+    ).astype(f32)
+    _, first_pull = jax.vjp(layer_norm, inputs, first_gain, first_shift)
+    d_norm_one, d_first_gain, d_first_shift = first_pull(d_normed)
+    grad_hidden = d_residual + d_norm_one
+
+    def scattered(grad):
+        return lax.psum_scatter(grad.astype(bf16), "rows", scatter_dimension=0, tiled=True)
+
+    def both(part):
+        return lax.all_gather(part, "blk", axis=0).astype(f32)
+
+    down_share = both(scattered(grad_down)).reshape(pieces * units, width)
+    up_share = both(scattered(grad_up)).reshape(pieces, -1, shards, units)
+    up_share = up_share.transpose(1, 2, 0, 3).reshape(-1, pieces * shards * units)
+    qkv_share = both(scattered(grad_qkv)).reshape(pieces, -1, 3, cols)
+    qkv_share = qkv_share.transpose(1, 2, 0, 3).reshape(-1, 3 * pieces * cols)
+    out_share = lax.psum(scattered(grad_out), "blk").astype(f32)
+    d_bias_own = jnp.sum(d_up.astype(f32), axis=0)
+    slots = jnp.zeros((shards, pieces, units), f32)
+    d_bias = lax.dynamic_update_index_in_dim(slots, d_bias_own.reshape(shards, units), piece, 1)
+    small = lax.psum(
+        (d_first_gain, d_first_shift, d_second_gain, d_second_shift, d_bias.reshape(-1)),
+        ("rows", "blk"),
+    )
+    return (output[None], grad_hidden[None], qkv_share, out_share, up_share, down_share) + small
+
+
+def splits_evenly(mesh):
+    pieces = mesh.shape["blk"]
+    return HEADS % pieces == 0 and HEADS // pieces * HEAD_DIM % 128 == 0
+
+
 def solution(mesh):
     in_specs = (
         P("rows", "blk", None),
@@ -280,6 +405,7 @@
         P(),
         P(),
     )
+    layer = split_layer if splits_evenly(mesh) else on_device
     return jax.shard_map(
-        on_device, mesh=mesh, in_specs=in_specs, out_specs=out_specs, check_vma=False
-    )
+        layer, mesh=mesh, in_specs=in_specs, out_specs=out_specs, check_vma=False
+    )

time: 1090 us -> 883 us (0.81)
  waiting for transfers between devices: 702 us -> 511 us
  matrix products: 206 us -> 170 us
  blocking collectives: 41.2 us -> 73.3 us
  other arithmetic: 54.4 us -> 38.2 us
    reduce_scatter x2 -> x7, waiting for transfers between devices: 351 us -> 251 us  [the longest x4 200 us: scattered(): lax.psum_scatter(grad.astype(bf16), 'rows', scatter_dimension=0, tiled=True)]
    all_gather x6 -> x7, waiting for transfers between devices: 310 us -> 236 us  [the longest x1 66.3 us: split_layer(): down_all = lax.all_gather(down_own, 'rows', axis=0, tiled=True)]
    dot_general x33 -> x18, matrix products: 206 us -> 170 us  [the longest x1 25.6 us: split_layer(): up_values = jnp.dot(second, up_all, preferred_element_type=f32) + bias_own]
    all_gather x0 -> x3, blocking collectives: none -> 32.2 us  [both(): return lax.all_gather(part, 'blk', axis=0).astype(f32)]
    reshape x0 -> x12, local copies, waits for them, and re-layouts: none -> 28.9 us  [the longest x3 11.4 us: split_layer(): up_share.transpose(1, 2, 0, 3).reshape(-1, pieces * shards * units)]
    all_to_all x0 -> x2, waiting for transfers between devices: none -> 22.6 us  [the longest x1 13.3 us: split_layer(): attended_low = lax.all_to_all(attended_part, 'blk', 0, 1, tiled=True)]
    unnamed x13 -> x15, waiting for transfers between devices: 24.5 us -> 1.91 us
    concatenate x1 -> x0, other arithmetic: 21.7 us -> none  [on_device(): jnp.concatenate([jnp.einsum('tc,tn->cn', normed_low, d_packed, preferred_...]
  transfers between devices with their start and end apart: 11 -> 17, of which waited for: 9 -> 14; matrix products, arithmetic and copies ran while one was open for 18% -> 25% of each run, Pallas kernels for 0% -> 0%
where the time goes in v1:
time: 883 us; the launch traced here: 879 us
  waiting for transfers between devices  511 us (58%)
  matrix products  170 us (19%)
  blocking collectives  73.3 us (8%)
  local copies, waits for them, and re-layouts  61.8 us (7%)
  other arithmetic  38.2 us (4%)
  between operations  14.6 us (2%)
  starting transfers between devices  10.2 us (1%)
    reduce_scatter x4, waiting for transfers between devices, scattered(): lax.psum_scatter(grad.astype(bf16), 'rows', scatter_dimension=0, tiled=True)  200 us
    all_gather x1, waiting for transfers between devices, split_layer(): down_all = lax.all_gather(down_own, 'rows', axis=0, tiled=True)  66.3 us
    all_gather x1, waiting for transfers between devices, split_layer(): up_all = lax.all_gather(up_own, 'rows', axis=0, tiled=True)  66.1 us
    all_gather x1, waiting for transfers between devices, split_layer(): qkv_all = lax.all_gather(qkv_own, 'rows', axis=0, tiled=True)  53.1 us
    psum x1, blocking collectives, split_layer(): lax.psum((d_first_gain, d_first_shift, d_second_gain, d_second_shift, d_b...  41.2 us
    all_gather x3, blocking collectives, both(): return lax.all_gather(part, 'blk', axis=0).astype(f32)  32.2 us
    reduce_scatter x1, waiting for transfers between devices, split_layer(): lax.psum_scatter(down_part, 'blk', scatter_dimension=0, tiled=True)  31.4 us
    all_gather x1, waiting for transfers between devices, split_layer(): hidden_all = lax.all_gather(hidden[0], 'blk', axis=0, tiled=True)  29.4 us
  transfers between devices with their start and end apart: 17, of which 14 were waited for; matrix products, arithmetic and copies ran while one was open for 25% of the time, Pallas kernels for 0%

profile of v1, /device:TPU:0, one launch (start us, length us, event | category | flops | bytes accessed | tf_op | source)
XLA Modules:
  0.0 879.0 jit_solution(3700643187208334247)
XLA Ops:
  14.6 29.4 %all-gather.23.cloned.1.call-done = bf16[1,768,1280]{2,1,0:T(8,128)(2,1)} async-done(((bf16[1,384,1280]{2,1,0:T(8,128)(2,1)}), bf16[1,768,1280]{2,1,0:T(8,128)(2,1)}) %all-gather.23.cloned.1.call-update) | async-done | bytes 1966096 | tf_op jit(solution)/shard_map/all_gather | solution.py:280
  48.1 53.1 %all-gather.13.cloned.1.call-done = bf16[1280,1920]{1,0:T(8,128)(2,1)} async-done(((bf16[80,1920]{1,0:T(8,128)(2,1)}), bf16[1280,1920]{1,0:T(8,128)(2,1)}) %all-gather.13.cloned.1.call-update) | async-done | bytes 4915216 | tf_op jit(solution)/shard_map/all_gather | solution.py:282
  112.8 9.8 %fusion.2 = (f32[10,768]{1,0:T(8,128)S(1)}, f32[10,768,768]{1,2,0:T(8,128)}) fusion(pred[768,768]{0,1:T(8,128)(4,1)S(1)} %broadcast_compare_fusion, bf16[10,768,64]{1,2,0:T(8,128)(2,1)S(1)} %bitcast.149, bf16[10,768,64]{1,2,0:T(8,128)(2,1)S(1)} %bitcast.147), kind=kOutput, calls=%fused_computation.7 | convolution fusion | flops 772661760 | bytes 26179584 | tf_op jit(solution)/shard_map/hqe,hke->hqk/dot_general | solution.py:297
  124.2 11.0 %fusion = f32[10,768]{1,0:T(8,128)S(1)} fusion(f32[10,768,768]{1,2,0:T(8,128)} %get-tuple-element.35, f32[10,768]{1,0:T(8,128)S(1)} %get-tuple-element.34, pred[768,768]{0,1:T(8,128)(4,1)S(1)} %broadcast_compare_fusion), kind=kLoop, calls=%fused_computation.5 | loop fusion | flops 23585280 | bytes 24244224 | tf_op jit(solution)/shard_map/reduce_sum | solution.py:301
  135.2 10.9 %fusion.6 = f32[10,768,64]{1,2,0:T(8,128)S(1)} fusion(bf16[10,768,64]{1,2,0:T(8,128)(2,1)S(1)} %bitcast.156, f32[10,768,768]{1,2,0:T(8,128)} %get-tuple-element.35, f32[10,768]{1,0:T(8,128)S(1)} %fusion, f32[10,768]{1,0:T(8,128)S(1)} %get-tuple-element.34, pred[768,768]{0,1:T(8,128)(4,1)S(1)} %broadcast_compare_fusion), kind=kOutput, calls=%fused_computation.11 | convolution fusion | flops 784465920 | bytes 27193344 | tf_op jit(solution)/shard_map/hqk,hke->hqe/dot_general | solution.py:303
  152.7 13.3 %all-to-all-done = bf16[2,384,640]{1,2,0:T(8,128)(2,1)S(1)} async-done(((bf16[2,384,640]{1,2,0:T(8,128)(2,1)}), bf16[2,384,640]{1,2,0:T(8,128)(2,1)S(1)}, u32[]{:S(2)}, u32[]{:S(2)}) %all-to-all-start) | async-done | bytes 983072 | tf_op jit(solution)/shard_map/all_to_all | solution.py:307
  187.4 14.9 %all-gather.17.cloned.1.call-done = bf16[768,1280]{1,0:T(8,128)(2,1)} async-done(((bf16[384,1280]{1,0:T(8,128)(2,1)}), bf16[768,1280]{1,0:T(8,128)(2,1)}) %all-gather.17.cloned.1.call-update) | async-done | bytes 1966096 | tf_op jit(solution)/shard_map/all_gather | solution.py:311
  202.4 66.1 %all-gather.19.cloned.1.call-done = bf16[1280,2560]{1,0:T(8,128)(2,1)} async-done(((bf16[80,2560]{1,0:T(8,128)(2,1)}), bf16[1280,2560]{1,0:T(8,128)(2,1)}) %all-gather.19.cloned.1.call-update) | async-done | bytes 6553616 | tf_op jit(solution)/shard_map/all_gather | solution.py:284
  268.5 25.6 %multiply_convert_fusion.1 = (bf16[768,2560]{1,0:T(8,128)(2,1)}, f32[768,2560]{1,0:T(8,128)}, f32[768,2560]{1,0:T(8,128)}) fusion(f32[2560]{0:T(1024)S(1)} %add.135, bf16[768,1280]{1,0:T(8,128)(2,1)} %all-gather.17.cloned.1.call-done, bf16[1280,2560]{1,0:T(8,128)(2,1)} %all-gather.19.cloned.1.call-done), kind=kOutput, calls=%fused_computation.25 | convolution fusion | flops 5162926080 | bytes 28190720 | tf_op jit(solution)/shard_map/dot_general | solution.py:312
  300.1 66.3 %all-gather.21.cloned.1.call-done = bf16[2560,1280]{1,0:T(8,128)(2,1)} async-done(((bf16[160,1280]{1,0:T(8,128)(2,1)}), bf16[2560,1280]{1,0:T(8,128)(2,1)}) %all-gather.21.cloned.1.call-update) | async-done | bytes 6553616 | tf_op jit(solution)/shard_map/all_gather | solution.py:285
  366.4 13.6 %convert_reduce_fusion = (f32[2560]{0:T(1024)S(1)}, bf16[768,2560]{1,0:T(8,128)(2,1)S(1)}) fusion(f32[768,2560]{1,0:T(8,128)} %get-tuple-element.27, bf16[2560,1280]{1,0:T(8,128)(2,1)} %all-gather.21.cloned.1.call-done, bf16[1,768,1280]{2,1,0:T(8,128)(2,1)} %all-gather.25.cloned.1.call-done, f32[768,2560]{1,0:T(8,128)} %get-tuple-element.38, f32[2560]{0:T(1024)S(1)} %add.135), kind=kOutput, calls=%fused_computation.24 | convolution fusion | flops 5066585600 | bytes 28200960 | tf_op jit(solution)/shard_map/tc,fc->tf/dot_general | solution.py:320
  388.9 9.8 %convolution_convert_fusion.5 = bf16[768,1280]{1,0:T(8,128)(2,1)} fusion(bf16[768,2560]{1,0:T(8,128)(2,1)} %get-tuple-element.26, bf16[2560,1280]{1,0:T(8,128)(2,1)} %all-gather.21.cloned.1.call-done), kind=kOutput, calls=%fused_computation.51 | convolution fusion | flops 5034147840 | bytes 12451840 | tf_op jit(solution)/shard_map/dot_general | solution.py:314
  398.8 18.7 %reduce-scatter.10.cloned.1.call-done = bf16[384,1280]{1,0:T(8,128)(2,1)} async-done(((bf16[768,1280]{1,0:T(8,128)(2,1)}), bf16[384,1280]{1,0:T(8,128)(2,1)}) %reduce-scatter.10.cloned.1.call-update) | async-done | bytes 983056 | tf_op jit(solution)/shard_map/reduce_scatter | solution.py:325
  419.4 31.4 %reduce-scatter.8.cloned.1.call-done = bf16[384,1280]{1,0:T(8,128)(2,1)} async-done(((bf16[768,1280]{1,0:T(8,128)(2,1)}), bf16[384,1280]{1,0:T(8,128)(2,1)}) %reduce-scatter.8.cloned.1.call-update) | async-done | bytes 983056 | tf_op jit(solution)/shard_map/reduce_scatter | solution.py:315
  487.8 15.6 %multiply_convert_fusion = bf16[10,768,768]{1,2,0:T(8,128)(2,1)} fusion(f32[10,768,768]{1,2,0:T(8,128)} %get-tuple-element.35, f32[10,768]{1,0:T(8,128)S(1)} %multiply_reduce_fusion, f32[10,768]{1,0:T(8,128)S(1)} %log_add_fusion, pred[768,768]{0,1:T(8,128)(4,1)S(1)} %broadcast_compare_fusion, bf16[10,768,64]{1,2,0:T(8,128)(2,1)} %bitcast.157, ...), kind=kOutput, calls=%fused_computation | convolution fusion | flops 796262400 | bytes 38006784 | tf_op jit(solution)/shard_map/hqe,hke->hqk/dot_general | solution.py:338
  515.7 11.6 %fusion.42 = bf16[10,64,768]{2,1,0:T(8,128)(2,1)S(1)} fusion(f32[10,768,768]{1,2,0:T(8,128)} %get-tuple-element.35, f32[10,768]{1,0:T(8,128)S(1)} %log_add_fusion, pred[768,768]{0,1:T(8,128)(4,1)S(1)} %broadcast_compare_fusion, bf16[768,10,64]{0,2,1:T(8,128)(2,1)S(1)} %copy-done.13), kind=kOutput, calls=%fused_computation.90 | convolution fusion | flops 784957440 | bytes 26179584 | tf_op jit(solution)/shard_map/hqk,hqe->khe/dot_general | solution.py:342
  539.0 10.5 %convolution_convert_fusion = bf16[2560,1280]{1,0:T(8,128)(2,1)} fusion(bf16[768,2560]{1,0:T(8,128)(2,1)} %get-tuple-element.26, bf16[1,768,1280]{2,1,0:T(8,128)(2,1)S(1)} %copy-done.31), kind=kOutput, calls=%fused_computation.12 | convolution fusion | flops 5036441600 | bytes 12451840 | tf_op jit(solution)/shard_map/tf,tn->fn/dot_general | solution.py:319
  551.1 9.4 %convolution_convert_fusion.1 = bf16[1280,2560]{1,0:T(8,128)(2,1)} fusion(bf16[768,1280]{1,0:T(8,128)(2,1)S(1)} %copy-done.30, bf16[768,2560]{1,0:T(8,128)(2,1)} %copy-done.35), kind=kOutput, calls=%fused_computation.13 | convolution fusion | flops 5036441600 | bytes 12451840 | tf_op jit(solution)/shard_map/tc,tn->cn/dot_general | solution.py:323
  576.7 41.2 %all-reduce = (f32[1280]{0:T(1024)}, f32[1280]{0:T(1024)}, f32[1280]{0:T(1024)}, f32[1280]{0:T(1024)}, f32[5120]{0:T(1024)}) all-reduce(f32[1280]{0:T(1024)S(1)} %get-tuple-element.13, f32[1280]{0:T(1024)S(1)} %get-tuple-element.17, f32[1280]{0:T(1024)S(1)} %get-tuple-element.11, ...), channel_id=1, replica_groups=mesh['rows'=16,'blk'=2] {'rows','blk'}, use_global_device_ids=true, to_apply=%region_23.24 | all-reduce | flops 10240 | bytes 81920 | tf_op jit(solution)/shard_map/psum | solution.py:368
  623.8 63.4 %reduce-scatter.20.cloned.1.call-done = bf16[160,1280]{1,0:T(8,128)(2,1)} async-done(((bf16[2560,1280]{1,0:T(8,128)(2,1)}), bf16[160,1280]{1,0:T(8,128)(2,1)}) %reduce-scatter.20.cloned.1.call-update) | async-done | bytes 409616 | tf_op jit(solution)/shard_map/reduce_scatter | solution.py:354
  687.2 11.6 %all-gather.4 = bf16[320,1280]{1,0:T(8,128)(2,1)S(1)} all-gather(bf16[160,1280]{1,0:T(8,128)(2,1)} %reduce-scatter.20.cloned.1.call-done), channel_id=6, replica_groups=mesh['rows'=16,'blk'=2] {'blk'}, dimensions={0}, use_global_device_ids=true | all-gather | bytes 1228800 | tf_op jit(solution)/shard_map/all_gather | solution.py:357
  700.1 77.4 %reduce-scatter.18.cloned.1.call-done = bf16[80,2560]{1,0:T(8,128)(2,1)} async-done(((bf16[1280,2560]{1,0:T(8,128)(2,1)}), bf16[80,2560]{1,0:T(8,128)(2,1)}) %reduce-scatter.18.cloned.1.call-update) | async-done | bytes 409616 | tf_op jit(solution)/shard_map/reduce_scatter | solution.py:354
  777.5 11.7 %all-gather.3 = bf16[160,2560]{1,0:T(8,128)(2,1)S(1)} all-gather(bf16[80,2560]{1,0:T(8,128)(2,1)} %reduce-scatter.18.cloned.1.call-done), channel_id=5, replica_groups=mesh['rows'=16,'blk'=2] {'blk'}, dimensions={0}, use_global_device_ids=true | all-gather | bytes 1228800 | tf_op jit(solution)/shard_map/all_gather | solution.py:357
  800.6 57.1 %reduce-scatter.14.cloned.1.call-done = bf16[80,1920]{1,0:T(8,128)(2,1)} async-done(((bf16[1280,1920]{1,0:T(8,128)(2,1)}), bf16[80,1920]{1,0:T(8,128)(2,1)}) %reduce-scatter.14.cloned.1.call-update) | async-done | bytes 307216 | tf_op jit(solution)/shard_map/reduce_scatter | solution.py:354
  (177 shorter events, 180.7 us)
Async XLA Ops:
  7.2 178.9 %copy-start = (bf16[320,1280]{1,0:T(8,128)(2,1)S(1)}, bf16[320,1280]{1,0:T(8,128)(2,1)}, u32[]{:S(2)}) copy-start(bf16[320,1280]{1,0:T(8,128)(2,1)} %param.22) | copy-start | bytes 2457604
  7.2 94.0 %copy-start.19 = (f32[1280]{0:T(1024)S(1)}, f32[1280]{0:T(1024)}, u32[]{:S(2)}) copy-start(f32[1280]{0:T(1024)} %param.14) | copy-start | bytes 15364
  7.2 94.0 %copy-start.32 = (f32[1280]{0:T(1024)S(1)}, f32[1280]{0:T(1024)}, u32[]{:S(2)}) copy-start(f32[1280]{0:T(1024)} %param.15) | copy-start | bytes 15364
  7.2 36.8 %all-gather.23.cloned.1.call-start = ((), (), s32[]{:S(2)}) async-start(), calls=%async_computation.22 | async-start | bytes 2949120 | tf_op jit(solution)/shard_map/all_gather | solution.py:280
  8.0 93.3 %all-gather.13.cloned.1.call-start = ((), (), s32[]{:S(2)}) async-start(), calls=%async_computation.9 | async-start | bytes 5222400 | tf_op jit(solution)/shard_map/all_gather | solution.py:282
  12.7 140.0 %all-gather.15.cloned.1.call-start = ((), (), s32[]{:S(2)}) async-start(), calls=%async_computation.10 | async-start | bytes 3481600 | tf_op jit(solution)/shard_map/all_gather | solution.py:283
  45.9 62.8 %copy-start.23 = (f32[768]{0:T(1024)}, f32[768]{0:T(1024)S(1)}, u32[]{:S(2)}) copy-start(f32[768]{0:T(1024)S(1)} %broadcast_multiply_fusion) | copy-start | bytes 9220
  48.1 60.6 %copy-start.26 = (f32[768]{0:T(1024)}, f32[768]{0:T(1024)S(1)}, u32[]{:S(2)}) copy-start(f32[768]{0:T(1024)S(1)} %add_rsqrt_fusion) | copy-start | bytes 9220
  148.8 17.2 %all-to-all-start = ((bf16[2,384,640]{1,2,0:T(8,128)(2,1)}), bf16[2,384,640]{1,2,0:T(8,128)(2,1)S(1)}, u32[]{:S(2)}, u32[]{:S(2)}) async-start(bf16[2,384,640]{1,2,0:T(8,128)(2,1)} %copy.81), calls=%async_computation | async-start | bytes 1966080 | tf_op jit(solution)/shard_map/all_to_all | solution.py:307
  152.4 50.0 %all-gather.17.cloned.1.call-start = ((), (), s32[]{:S(2)}) async-start(), calls=%async_computation.11 | async-start | bytes 2949120 | tf_op jit(solution)/shard_map/all_gather | solution.py:311
  172.8 95.7 %all-gather.19.cloned.1.call-start = ((), (), s32[]{:S(2)}) async-start(), calls=%async_computation.12 | async-start | bytes 6963200 | tf_op jit(solution)/shard_map/all_gather | solution.py:284
  185.4 114.7 %all-gather.25.cloned.1.call-start = ((), (), s32[]{:S(2)}) async-start(), calls=%async_computation.23 | async-start | bytes 2949120 | tf_op jit(solution)/shard_map/all_gather | solution.py:281
  186.0 180.4 %all-gather.21.cloned.1.call-start = ((), (), s32[]{:S(2)}) async-start(), calls=%async_computation.13 | async-start | bytes 6963200 | tf_op jit(solution)/shard_map/all_gather | solution.py:285
  186.9 230.6 %reduce-scatter.10.cloned.1.call-start = ((), (), s32[]{:S(2)}) async-start(), calls=%async_computation.15 | async-start | bytes 2949120 | tf_op jit(solution)/shard_map/reduce_scatter | solution.py:325
  388.4 62.4 %reduce-scatter.8.cloned.1.call-start = ((), (), s32[]{:S(2)}) async-start(), calls=%async_computation.14 | async-start | bytes 2949120 | tf_op jit(solution)/shard_map/reduce_scatter | solution.py:315
  461.9 17.6 %all-to-all-start.1 = ((bf16[384,2,640]{0,2,1:T(8,128)(2,1)}), bf16[384,2,640]{0,2,1:T(8,128)(2,1)}, u32[]{:S(2)}, u32[]{:S(2)}) async-start(bf16[384,2,640]{0,2,1:T(8,128)(2,1)} %bitcast.17), calls=%async_computation.3 | async-start | bytes 1966080 | tf_op jit(solution)/shard_map/all_to_all | solution.py:334
  466.3 72.6 %reduce-scatter.16.cloned.1.call-start = ((), (), s32[]{:S(2)}) async-start(), calls=%async_computation.18 | async-start | bytes 3481600 | tf_op jit(solution)/shard_map/reduce_scatter | solution.py:354
  470.0 102.4 %reduce-scatter.12.cloned.1.call-start = ((), (), s32[]{:S(2)}) async-start(), calls=%async_computation.16 | async-start | bytes 2949120 | tf_op jit(solution)/shard_map/reduce_scatter | solution.py:346
  536.4 85.7 %all-reduce.3.cloned.1.call-start = ((), (), s32[]{:S(2)}) async-start(), calls=%async_computation.19 | async-start | bytes 409600 | tf_op jit(solution)/shard_map/psum | solution.py:364
  539.0 148.2 %reduce-scatter.20.cloned.1.call-start = ((), (), s32[]{:S(2)}) async-start(), calls=%async_computation.21 | async-start | bytes 6963200 | tf_op jit(solution)/shard_map/reduce_scatter | solution.py:354
  549.5 228.0 %reduce-scatter.18.cloned.1.call-start = ((), (), s32[]{:S(2)}) async-start(), calls=%async_computation.20 | async-start | bytes 6963200 | tf_op jit(solution)/shard_map/reduce_scatter | solution.py:354
  560.5 297.3 %reduce-scatter.14.cloned.1.call-start = ((), (), s32[]{:S(2)}) async-start(), calls=%async_computation.17 | async-start | bytes 5222400 | tf_op jit(solution)/shard_map/reduce_scatter | solution.py:354
  570.7 47.2 %copy-start.7 = (bf16[1,384,1280]{2,1,0:T(8,128)(2,1)S(1)}, bf16[1,384,1280]{2,1,0:T(8,128)(2,1)}, u32[]{:S(2)}) copy-start(bf16[1,384,1280]{2,1,0:T(8,128)(2,1)} %param.23) | copy-start | bytes 2949124
  794.6 77.6 %copy-start.1 = (bf16[320,1280]{1,0:T(8,128)(2,1)S(1)}, bf16[320,1280]{1,0:T(8,128)(2,1)}, u32[]{:S(2)}) copy-start(bf16[320,1280]{1,0:T(8,128)(2,1)} %param.22) | copy-start | bytes 2457604
  (29 other events, 193.4 us)
Sparse Core Ops, SparseCore 0:
  9.6 34.3 all-gather.22
  46.7 54.4 all-gather.12
  103.5 44.3 all-gather.14
  172.9 29.4 all-gather.16
  205.1 63.3 all-gather.18
  269.9 30.1 all-gather.24
  303.0 63.3 all-gather.20
  388.5 28.9 reduce-scatter.9
  420.4 30.3 reduce-scatter.7
  470.7 68.2 reduce-scatter.15
  541.9 29.3 reduce-scatter.11
  573.4 22.7 all-reduce.2
  600.1 87.0 reduce-scatter.19
  691.5 85.9 reduce-scatter.17
  781.3 76.3 reduce-scatter.13

commit v2 on v1

--- a/solution.py
+++ b/solution.py
@@ -3,6 +3,8 @@
 import jax
 import jax.numpy as jnp
 from jax import lax
+from jax.experimental import pallas as pl
+from jax.experimental.pallas import tpu as pltpu
 from jax.sharding import PartitionSpec as P
 
 HEADS = 20
@@ -252,6 +254,426 @@
     )
 
 
+MESH = pl.DeviceIdType.MESH
+ROWS_Z, ROWS_Y = 4, 2
+PAIR = 128
+
+
+def place_of():
+    index = lax.axis_index("rows")
+    return index // 4, lax.rem(index // 2, 2), lax.rem(index, 2)
+
+
+def row_of(z, y, core):
+    return (lax.rem(z + ROWS_Z, ROWS_Z) * ROWS_Y + y) * 2 + core
+
+
+def aligned(index, step):
+    return pl.ds(pl.multiple_of(index * step, step), step)
+
+
+def dot_nt(left, right):
+    return lax.dot_general(left, right, (((1,), (1,)), ((), ())), preferred_element_type=jnp.float32)
+
+
+def dot_nn(left, right):
+    return jnp.dot(left, right, preferred_element_type=jnp.float32)
+
+
+def head_lanes(width):
+    lane = lax.broadcasted_iota(jnp.int32, (1, width), 1)
+    return (lane < HEAD_DIM, lane >= HEAD_DIM)
+
+
+def greet(peers):
+    barrier = pltpu.get_barrier_semaphore()
+    for peer in peers:
+        pl.semaphore_signal(barrier, inc=1, device_id=peer, device_id_type=MESH)
+    pl.semaphore_wait(barrier, len(peers))
+
+
+def neighbours():
+    z, y, core = place_of()
+    return [
+        {"rows": row_of(z + 1, y, core)},
+        {"rows": row_of(z + 2, y, core)},
+        {"rows": row_of(z + 3, y, core)},
+        {"rows": row_of(z, 1 - y, core)},
+        {"rows": row_of(z, y, 1 - core)},
+        {"blk": 1 - lax.axis_index("blk")},
+    ]
+
+
+def write_mask(starts_ref, mask_ref):
+    length = mask_ref.shape[0]
+    step = 128
+
+    def rows(i, carry):
+        key_at = lax.broadcasted_iota(jnp.int32, (step, length), 0) + i * step
+        query_at = lax.broadcasted_iota(jnp.int32, (step, length), 1)
+        key_seg = jnp.zeros((step, length), jnp.int32)
+        query_seg = jnp.zeros((step, length), jnp.int32)
+        for cell in range(starts_ref.shape[1]):
+            start = starts_ref[0, cell]
+            key_seg += (key_at >= start).astype(jnp.int32)
+            query_seg += (query_at >= start).astype(jnp.int32)
+        mask_ref[aligned(i, step), :] = jnp.where(key_seg == query_seg, 0.0, masked_score)
+        return carry
+
+    lax.fori_loop(0, length // step, rows, 0)
+
+
+def forward_kernel(
+    hidden, cot, starts, gain1, shift1, gain2, shift2, bias, q_own, o_own, u_own, d_own,
+    q_all, o_all, u_all, d_all, dy_all, normed_t_out, packed_out, lse_out, att_t_out, resid_out,
+    second_t_out, act_out, act_t_out, slope_out,
+    hid_other, normed, wq, wo, wu, packed, mask, att_part, att_own, resid, second,
+    act, act_t, slope, normed_t, att_t, second_t, lse,
+    local_sem, send_sem, recv_sem, x_send, x_recv,
+):
+    bf16 = jnp.bfloat16
+    z, y, core = place_of()
+    me = row_of(z, y, core)
+    piece = lax.axis_index("blk")
+    other = 1 - piece
+    own_rows, width = hidden.shape
+    length = packed.shape[0]
+    own = (q_own, o_own, u_own, d_own)
+    gathered = (q_all, o_all, u_all, d_all)
+    x_peer = {"blk": other}
+    peers = neighbours()
+    pairs = packed.shape[1] // (3 * PAIR)
+    waits = []
+
+    def local(src, dst, index):
+        return pltpu.make_async_copy(src, dst, local_sem.at[index])
+
+    def block(w, stage):
+        if stage < 3:
+            slot, peer = me, peers[stage]
+        elif stage < 7:
+            slot, peer = row_of(z - (stage - 3), y, core), peers[3]
+        elif stage < 11:
+            slot, peer = row_of(z - (stage - 7), y, core), peers[4]
+        else:
+            slot, peer = row_of(z - (stage - 11), 1 - y, core), peers[4]
+        src = own[w] if stage in (0, 1, 2, 3, 7) else gathered[w].at[slot]
+        index = w * 15 + stage
+        return pltpu.make_async_remote_copy(
+            src_ref=src, dst_ref=gathered[w].at[slot], send_sem=send_sem.at[index],
+            recv_sem=recv_sem.at[index], device_id=peer, device_id_type=MESH,
+        )
+
+    def start(w, *stages):
+        for stage in stages:
+            block(w, stage).start()
+
+    def arrived(w, *stages):
+        for stage in stages:
+            block(w, stage).wait_recv()
+
+    def to_x(src, dst, index):
+        return pltpu.make_async_remote_copy(
+            src_ref=src, dst_ref=dst, send_sem=x_send.at[index], recv_sem=x_recv.at[index],
+            device_id=x_peer, device_id_type=MESH,
+        )
+
+    def relay_z(w, k):
+        arrived(w, k - 1)
+        start(w, 3 + k, 7 + k)
+
+    def relay_y(w, k):
+        arrived(w, 3 + k)
+        start(w, 11 + k)
+
+    greet(peers)
+    for w in range(4):
+        start(w, 0, 2, 1)
+        start(w, 7)
+        if w == 0:
+            start(w, 3)
+    hidden_x = to_x(hidden, hid_other, 0)
+    hidden_x.start()
+    cot_x = to_x(cot, dy_all.at[piece], 1)
+    cot_x.start()
+    for w in range(4):
+        local(own[w], gathered[w].at[me], w).start()
+    local(cot, dy_all.at[piece], 4).start()
+
+    def norm_rows(read, half):
+        step = 64
+
+        def body(i, carry):
+            rows = read(aligned(i, step)).astype(jnp.float32)
+            low = layer_norm(rows, gain1[...], shift1[...]).astype(bf16)
+            normed[pl.ds(pl.multiple_of(half * own_rows + i * step, step), step), :] = low
+            return carry
+
+        lax.fori_loop(0, own_rows // step, body, 0)
+
+    norm_rows(lambda rows: hidden[rows, :], piece)
+    relay_z(0, 1)
+    relay_z(0, 3)
+    start(1, 3)
+    write_mask(starts, mask)
+    relay_y(0, 0)
+    relay_y(0, 1)
+    hidden_x.wait_recv()
+    norm_rows(lambda rows: hid_other[rows, :], other)
+    relay_z(0, 2)
+    relay_y(0, 3)
+
+    def flip(i, carry):
+        normed_t[aligned(i, 128), :] = normed[:, aligned(i, 128)].T
+        return carry
+
+    lax.fori_loop(0, width // 128, flip, 0)
+    local(normed_t, normed_t_out, 8).start()
+    relay_z(1, 1)
+    relay_y(0, 2)
+    relay_z(1, 3)
+    start(2, 3)
+    arrived(0, *range(7, 15))
+    local(own[0], gathered[0].at[me], 0).wait()
+    local(q_all, wq, 5).start()
+    local(q_all, wq, 5).wait()
+
+    def project(i, carry):
+        cols = aligned(i, 3 * PAIR)
+        weight = wq[:, :, cols].reshape(width, 3 * PAIR)
+        value = dot_nn(normed[...], weight).astype(bf16)
+        queries = pl.ds(pl.multiple_of(i * 3 * PAIR, PAIR), PAIR)
+        rest = pl.ds(pl.multiple_of(i * 3 * PAIR + PAIR, PAIR), 2 * PAIR)
+        packed[:, queries] = value[:, :PAIR] * jnp.asarray(HEAD_DIM ** (-0.5), bf16)
+        packed[:, rest] = value[:, PAIR:]
+        return carry
+
+    lax.fori_loop(0, pairs, project, 0)
+    local(packed, packed_out, 9).start()
+    first_lanes = head_lanes(PAIR)
+
+    def attend(p):
+        base = 3 * PAIR * p
+        value_t = packed[:, base + 2 * PAIR : base + 3 * PAIR].T
+        step = 256
+
+        def rows(i, carry):
+            queries = packed[aligned(i, step), base : base + PAIR]
+            keys = packed[:, base + PAIR : base + 2 * PAIR]
+            halves = []
+            for h in range(2):
+                one = jnp.where(first_lanes[h], queries, jnp.zeros_like(queries))
+                scores = dot_nt(keys, one) + mask[:, aligned(i, step)]
+                top = jnp.max(scores, axis=0, keepdims=True)
+                weights = jnp.exp(scores - top)
+                total = jnp.sum(weights, axis=0, keepdims=True)
+                lse[2 * p + h : 2 * p + h + 1, aligned(i, step)] = top + jnp.log(total)
+                summed = dot_nn(value_t[h * HEAD_DIM : (h + 1) * HEAD_DIM], weights.astype(bf16))
+                halves.append(summed / total)
+            both = jnp.concatenate(halves, axis=0).T.astype(bf16)
+            att_part[aligned(i, step), p * PAIR : (p + 1) * PAIR] = both
+            return carry
+
+        lax.fori_loop(0, length // step, rows, 0)
+
+    def att_cols(half, p):
+        return pl.ds(pl.multiple_of(half * pairs * PAIR + p * PAIR, PAIR), PAIR)
+
+    att_x = []
+    for p in range(pairs):
+        attend(p)
+        part = att_part.at[pl.ds(pl.multiple_of(other * own_rows, 128), own_rows), pl.ds(p * PAIR, PAIR)]
+        att_x.append(to_x(part, att_own.at[:, att_cols(piece, p)], 2 + p))
+        att_x[-1].start()
+        mine = att_part[pl.ds(pl.multiple_of(piece * own_rows, 128), own_rows), p * PAIR : (p + 1) * PAIR]
+        att_own[:, att_cols(piece, p)] = mine
+        if p == 0:
+            relay_y(1, 0)
+            relay_y(1, 1)
+        elif p == 1:
+            relay_z(1, 2)
+        elif p == 2:
+            relay_y(1, 3)
+        elif p == 3:
+            relay_z(2, 1)
+        elif p == 4:
+            relay_y(1, 2)
+    local(lse, lse_out, 10).start()
+    for copy in att_x:
+        copy.wait_recv()
+    arrived(1, *range(7, 15))
+    local(own[1], gathered[1].at[me], 1).wait()
+    local(o_all, wo, 6).start()
+
+    def flip_att(i, carry):
+        att_t[aligned(i, 128), :] = att_own[:, aligned(i, 128)].T
+        return carry
+
+    lax.fori_loop(0, width // 128, flip_att, 0)
+    local(att_t, att_t_out, 11).start()
+    relay_z(2, 3)
+    start(3, 3)
+    local(o_all, wo, 6).wait()
+
+    def merge(i, carry):
+        cols = aligned(i, 256)
+        weight = wo[:, :, cols].reshape(width, 256)
+        resid[:, cols] = hidden[:, cols].astype(jnp.float32) + dot_nn(att_own[...], weight)
+        return carry
+
+    lax.fori_loop(0, width // 256, merge, 0)
+    local(resid, resid_out, 12).start()
+
+    def second_rows(i, carry):
+        rows = aligned(i, 64)
+        second[piece, rows, :] = layer_norm(resid[rows, :], gain2[...], shift2[...]).astype(bf16)
+        return carry
+
+    lax.fori_loop(0, own_rows // 64, second_rows, 0)
+    second_x = to_x(second.at[piece], second.at[piece], 2 + pairs)
+    second_x.start()
+    relay_y(2, 0)
+    relay_y(2, 1)
+    relay_z(2, 2)
+    second_x.wait_recv()
+
+    def flip_second(i, carry):
+        cols = aligned(i, 128)
+        second_t[cols, :] = second[:, :, cols].reshape(length, 128).T
+        return carry
+
+    lax.fori_loop(0, width // 128, flip_second, 0)
+    local(second_t, second_t_out, 13).start()
+    relay_y(2, 3)
+    relay_z(3, 1)
+    relay_y(2, 2)
+    arrived(2, *range(7, 15))
+    local(own[2], gathered[2].at[me], 2).wait()
+    local(u_all, wu, 7).start()
+    local(u_all, wu, 7).wait()
+    relay_z(3, 3)
+    unit = 256
+    steps = act.shape[1] // unit
+
+    def expand(i, carry):
+        cols = aligned(i // 2, unit)
+        rows = aligned(lax.rem(i, 2), own_rows)
+        weight = wu[:, :, cols].reshape(width, unit)
+        up = dot_nn(second[lax.rem(i, 2)], weight) + bias[:, cols]
+        cdf = 0.5 * (1.0 + lax.erf(up * (0.5 ** 0.5)))
+        pdf = jnp.exp(up * up * -0.5) * ((2.0 * math.pi) ** -0.5)
+        value = (up * cdf).astype(bf16)
+        act[rows, cols] = value
+        act_t[cols, rows] = value.T
+        slope[rows, cols] = (cdf + up * pdf).astype(bf16)
+        return carry
+
+    lax.fori_loop(0, steps, expand, 0)
+    relay_y(3, 0)
+    relay_y(3, 1)
+    lax.fori_loop(steps, 2 * steps, expand, 0)
+    local(act, act_out, 14).start()
+    local(act_t, act_t_out, 15).start()
+    local(slope, slope_out, 16).start()
+    relay_z(3, 2)
+    relay_y(3, 3)
+    relay_y(3, 2)
+    arrived(3, *range(7, 15))
+    cot_x.wait_recv()
+    local(own[3], gathered[3].at[me], 3).wait()
+    local(cot, dy_all.at[piece], 4).wait()
+    local(normed_t, normed_t_out, 8).wait()
+    local(packed, packed_out, 9).wait()
+    local(lse, lse_out, 10).wait()
+    local(att_t, att_t_out, 11).wait()
+    local(resid, resid_out, 12).wait()
+    local(second_t, second_t_out, 13).wait()
+    local(act, act_out, 14).wait()
+    local(act_t, act_t_out, 15).wait()
+    local(slope, slope_out, 16).wait()
+    for w in range(4):
+        for stage in range(15):
+            block(w, stage).wait_send()
+    for copy in [hidden_x, cot_x, second_x] + att_x:
+        copy.wait_send()
+
+
+def forward(hidden, cot, starts, gain1, shift1, gain2, shift2, bias, q_own, o_own, u_own, d_own):
+    own_rows, width = hidden.shape
+    length = 2 * own_rows
+    cols = q_own.shape[1]
+    units = u_own.shape[1]
+    bf16, f32 = jnp.bfloat16, jnp.float32
+    shards = lax.axis_size("rows")
+    weights = (q_own, o_own, u_own, d_own)
+    head_rows = 16
+    outs = [((shards,) + w.shape, bf16) for w in weights] + [
+        ((2, own_rows, width), bf16),
+        ((width, length), bf16),
+        ((length, cols), bf16),
+        ((head_rows, length), f32),
+        ((width, own_rows), bf16),
+        ((own_rows, width), f32),
+        ((width, length), bf16),
+        ((length, units), bf16),
+        ((units, length), bf16),
+        ((length, units), bf16),
+    ]
+    scratch = [
+        ((own_rows, width), bf16),
+        ((length, width), bf16),
+        ((shards,) + q_own.shape, bf16),
+        ((shards,) + o_own.shape, bf16),
+        ((shards,) + u_own.shape, bf16),
+        ((length, cols), bf16),
+        ((length, length), f32),
+        ((length, cols // 3), bf16),
+        ((own_rows, width), bf16),
+        ((own_rows, width), f32),
+        ((2, own_rows, width), bf16),
+        ((length, units), bf16),
+        ((units, length), bf16),
+        ((length, units), bf16),
+        ((width, length), bf16),
+        ((width, own_rows), bf16),
+        ((width, length), bf16),
+        ((head_rows, length), f32),
+    ]
+    vmem = pl.BlockSpec(memory_space=pltpu.VMEM)
+    anywhere = pl.BlockSpec(memory_space=pl.ANY)
+    smem = pl.BlockSpec(memory_space=pltpu.SMEM)
+    dma = pltpu.SemaphoreType.DMA
+    x_copies = 3 + cols // (3 * PAIR)
+    return pl.pallas_call(
+        forward_kernel,
+        out_shape=[jax.ShapeDtypeStruct(shape, kind) for shape, kind in outs],
+        in_specs=[vmem, anywhere, smem] + [vmem] * 5 + [anywhere] * 4,
+        out_specs=[anywhere] * len(outs),
+        scratch_shapes=[pltpu.VMEM(shape, kind) for shape, kind in scratch]
+        + [dma((17,)), dma((60,)), dma((60,)), dma((x_copies,)), dma((x_copies,))],
+        compiler_params=pltpu.CompilerParams(
+            collective_id=1, has_side_effects=True, vmem_limit_bytes=60 * 1024 * 1024
+        ),
+        name="forward",
+    )(hidden, cot, starts, gain1, shift1, gain2, shift2, bias, *weights)
+
+
+def own_shares(qkv_weight, up_weight, hidden_bias, down_weight, piece, pieces, shards, cols, units):
+    pairs = cols // PAIR
+    qkv_own = lax.dynamic_index_in_dim(
+        qkv_weight.reshape(-1, 3, pieces, pairs, PAIR), piece, 2, keepdims=False
+    )
+    qkv_own = qkv_own.transpose(0, 2, 1, 3).reshape(-1, 3 * cols)
+    up_own = lax.dynamic_index_in_dim(
+        up_weight.reshape(-1, shards, pieces, units), piece, 2, keepdims=False
+    ).reshape(-1, shards * units)
+    bias_own = lax.dynamic_index_in_dim(
+        hidden_bias.reshape(shards, pieces, units), piece, 1, keepdims=False
+    ).reshape(1, -1)
+    down_own = lax.dynamic_slice_in_dim(down_weight, piece * units, units, 0)
+    return qkv_own, up_own, bias_own, down_own
+
+
 def split_layer(
     hidden, starts, first_gain, first_shift, qkv_weight, out_weight, second_gain, second_shift,
     up_weight, hidden_bias, down_weight, cotangent,
@@ -262,65 +684,41 @@
     shards = lax.axis_size("rows")
     heads = HEADS // pieces
     cols = heads * HEAD_DIM
+    pairs = cols // PAIR
     length = own_rows * pieces
     units = down_weight.shape[0] // pieces
     scale = HEAD_DIM ** (-0.5)
-    starts_row = starts[0]
-
-    qkv_own = lax.dynamic_index_in_dim(
-        qkv_weight.reshape(-1, 3, pieces, cols), piece, 2, keepdims=False
-    ).reshape(-1, 3 * cols)
-    up_own = lax.dynamic_index_in_dim(
-        up_weight.reshape(-1, shards, pieces, units), piece, 2, keepdims=False
-    ).reshape(-1, shards * units)
-    bias_own = lax.dynamic_index_in_dim(
-        hidden_bias.reshape(shards, pieces, units), piece, 1, keepdims=False
-    ).reshape(-1)
-    down_own = lax.dynamic_slice_in_dim(down_weight, piece * units, units, 0)
-    hidden_all = lax.all_gather(hidden[0], "blk", axis=0, tiled=True)
-    dy_all = lax.all_gather(cotangent[0], "blk", axis=0, tiled=True)
-    qkv_all = lax.all_gather(qkv_own, "rows", axis=0, tiled=True)
-    out_all = lax.all_gather(out_weight, "rows", axis=0, tiled=True)
-    up_all = lax.all_gather(up_own, "rows", axis=0, tiled=True)
-    down_all = lax.all_gather(down_own, "rows", axis=0, tiled=True)
-
     f32 = jnp.float32
     bf16 = jnp.bfloat16
-    normed = layer_norm(hidden_all.astype(f32), first_gain, first_shift).astype(bf16)
-    packed = jnp.dot(normed, qkv_all, preferred_element_type=f32).astype(bf16)
-    q, k, v = (
-        packed[:, i * cols : (i + 1) * cols].reshape(length, heads, HEAD_DIM).transpose(1, 0, 2)
-        for i in range(3)
-    )
-    seg = segment_of(starts_row, jnp.arange(length, dtype=jnp.int32))
+    qkv_own, up_own, bias_own, down_own = own_shares(
+        qkv_weight, up_weight, hidden_bias, down_weight, piece, pieces, shards, cols, units
+    )
+    flat = lambda v: v.reshape(1, -1)
+    (
+        qkv_all, out_all, up_all, down_all, dy_all, normed_t, packed, lse, att_t, residual, second_t,
+        activated, activated_t, slope,
+    ) = forward(
+        hidden[0], cotangent[0], starts, flat(first_gain), flat(first_shift), flat(second_gain),
+        flat(second_shift), bias_own, qkv_own, out_weight, up_own, down_own,
+    )
+    qkv_all, out_all, up_all, down_all = (
+        w.reshape(-1, w.shape[-1]) for w in (qkv_all, out_all, up_all, down_all)
+    )
+    dy_all = dy_all.reshape(length, width)
+    triple = packed.reshape(length, pairs, 3, 2, HEAD_DIM)
+    q, k, v = (triple[:, :, i].reshape(length, heads, HEAD_DIM).transpose(1, 0, 2) for i in range(3))
+    seg = segment_of(starts[0], jnp.arange(length, dtype=jnp.int32))
     allowed = (seg[:, None] == seg[None, :])[None]
-    scores = jnp.einsum("hqe,hke->hqk", q, k, preferred_element_type=f32) * scale
-    scores = jnp.where(allowed, scores, masked_score)
-    top = jnp.max(scores, axis=-1, keepdims=True)
-    weights = jnp.exp(scores - top)
-    total = jnp.sum(weights, axis=-1, keepdims=True)
-    log_total = top + jnp.log(total)
-    attended = jnp.einsum(
-        "hqk,hke->hqe", (weights / total).astype(bf16), v, preferred_element_type=f32
-    )
-    attended_part = attended.transpose(1, 0, 2).reshape(length, cols).astype(bf16)
-    attended_low = lax.all_to_all(attended_part, "blk", 0, 1, tiled=True)
     inputs = hidden[0].astype(f32)
-    residual = inputs + jnp.dot(attended_low, out_all, preferred_element_type=f32)
-    second_own = layer_norm(residual, second_gain, second_shift).astype(bf16)
-    second = lax.all_gather(second_own, "blk", axis=0, tiled=True)
-    up_values = jnp.dot(second, up_all, preferred_element_type=f32) + bias_own
-    activated = jax.nn.gelu(up_values, approximate=False).astype(bf16)
     down_part = jnp.dot(activated, down_all, preferred_element_type=f32).astype(bf16)
     output = residual + lax.psum_scatter(
         down_part, "blk", scatter_dimension=0, tiled=True
     ).astype(f32)
 
-    grad_down = jnp.einsum("tf,tn->fn", activated, dy_all, preferred_element_type=f32)
+    grad_down = jnp.dot(activated_t, dy_all, preferred_element_type=f32)
     d_act = jnp.einsum("tc,fc->tf", dy_all, down_all, preferred_element_type=f32)
-    _, gelu_pull = jax.vjp(lambda u: jax.nn.gelu(u, approximate=False), up_values)
-    d_up = gelu_pull(d_act)[0].astype(bf16)
-    grad_up = jnp.einsum("tc,tn->cn", second, d_up, preferred_element_type=f32)
+    d_up = (d_act * slope.astype(f32)).astype(bf16)
+    grad_up = jnp.dot(second_t, d_up, preferred_element_type=f32)
     d_second_part = jnp.einsum("tf,cf->tc", d_up, up_all, preferred_element_type=f32)
     d_second = lax.psum_scatter(
         d_second_part.astype(bf16), "blk", scatter_dimension=0, tiled=True
@@ -329,19 +727,21 @@
     d_norm_two, d_second_gain, d_second_shift = second_pull(d_second)
     d_residual = cotangent[0].astype(f32) + d_norm_two
     d_branch = d_residual.astype(bf16)
-    grad_out = jnp.einsum("tc,tn->cn", attended_low, d_branch, preferred_element_type=f32)
+    grad_out = jnp.dot(att_t, d_branch, preferred_element_type=f32)
     d_att_own = jnp.einsum("tc,kc->tk", d_branch, out_all, preferred_element_type=f32)
     d_att = lax.all_to_all(d_att_own.astype(bf16), "blk", 1, 0, tiled=True)
     d_att3 = d_att.reshape(length, heads, HEAD_DIM).transpose(1, 0, 2)
-    row_dots = jnp.sum(d_att3.astype(f32) * attended, axis=-1, keepdims=True)
-    probs = jnp.where(allowed, jnp.exp(scores - log_total), 0.0)
+    scores = jnp.einsum("hqe,hke->hqk", q, k, preferred_element_type=f32)
+    probs = jnp.where(allowed, jnp.exp(scores - lse[:heads, :, None]), 0.0)
     d_probs = jnp.einsum("hqe,hke->hqk", d_att3, v, preferred_element_type=f32)
+    row_dots = jnp.sum(probs * d_probs, axis=-1, keepdims=True)
     d_scores = (probs * (d_probs - row_dots)).astype(bf16)
     dq = jnp.einsum("hqk,hke->qhe", d_scores, k, preferred_element_type=f32) * scale
-    dk = jnp.einsum("hqk,hqe->khe", d_scores, q, preferred_element_type=f32) * scale
+    dk = jnp.einsum("hqk,hqe->khe", d_scores, q, preferred_element_type=f32)
     dv = jnp.einsum("hqk,hqe->khe", probs.astype(bf16), d_att3, preferred_element_type=f32)
-    d_packed = jnp.concatenate([t.reshape(length, cols) for t in (dq, dk, dv)], axis=1).astype(bf16)
-    grad_qkv = jnp.einsum("tc,tn->cn", normed, d_packed, preferred_element_type=f32)
+    d_packed = jnp.stack([t.reshape(length, pairs, PAIR) for t in (dq, dk, dv)], axis=2)
+    d_packed = d_packed.reshape(length, 3 * cols).astype(bf16)
+    grad_qkv = jnp.dot(normed_t, d_packed, preferred_element_type=f32)
     d_normed_part = jnp.einsum("tn,cn->tc", d_packed, qkv_all, preferred_element_type=f32)
     d_normed = lax.psum_scatter(
         d_normed_part.astype(bf16), "blk", scatter_dimension=0, tiled=True
@@ -359,8 +759,8 @@
     down_share = both(scattered(grad_down)).reshape(pieces * units, width)
     up_share = both(scattered(grad_up)).reshape(pieces, -1, shards, units)
     up_share = up_share.transpose(1, 2, 0, 3).reshape(-1, pieces * shards * units)
-    qkv_share = both(scattered(grad_qkv)).reshape(pieces, -1, 3, cols)
-    qkv_share = qkv_share.transpose(1, 2, 0, 3).reshape(-1, 3 * pieces * cols)
+    qkv_share = both(scattered(grad_qkv)).reshape(pieces, -1, pairs, 3, PAIR)
+    qkv_share = qkv_share.transpose(1, 3, 0, 2, 4).reshape(-1, 3 * pieces * cols)
     out_share = lax.psum(scattered(grad_out), "blk").astype(f32)
     d_bias_own = jnp.sum(d_up.astype(f32), axis=0)
     slots = jnp.zeros((shards, pieces, units), f32)
@@ -374,7 +774,7 @@
 
 def splits_evenly(mesh):
     pieces = mesh.shape["blk"]
-    return HEADS % pieces == 0 and HEADS // pieces * HEAD_DIM % 128 == 0
+    return pieces == 2 and mesh.shape["rows"] == 2 * ROWS_Z * ROWS_Y and HEADS % (2 * pieces) == 0
 
 
 def solution(mesh):

time: 883 us -> 713 us (0.81)
  waiting for transfers between devices: 511 us -> 243 us
  Pallas kernels: 0 us -> 158 us
  matrix products: 170 us -> 115 us
    all_gather x7 -> x0, waiting for transfers between devices: 236 us -> none  [the longest x1 66.3 us: split_layer(): down_all = lax.all_gather(down_own, 'rows', axis=0, tiled=True)]
    pallas_call x0 -> x1, Pallas kernels: none -> 158 us  [forward(): pl.pallas_call(forward_kernel, out_shape=[jax.ShapeDtypeStruct(shape, kin...]
    dot_general x10 -> x6, matrix products: 99 us -> 46.2 us  [the longest x1 10.3 us: split_layer(): grad_down = jnp.dot(activated_t, dy_all, preferred_element_type=f32)]
    convert_element_type x2, other arithmetic: 1.44 us -> 18.1 us  [the longest x1 16.3 us: split_layer(): d_scores = (probs * (d_probs - row_dots)).astype(bf16)]
    reduce_scatter x1, waiting for transfers between devices: 18.7 us -> 3.65 us  [split_layer(): lax.psum_scatter(d_second_part.astype(bf16), 'blk', scatter_dimension=0,...]
    all_to_all x1 -> x0, waiting for transfers between devices: 13.3 us -> none  [split_layer(): attended_low = lax.all_to_all(attended_part, 'blk', 0, 1, tiled=True)]
    reduce_sum x2 -> x0, other arithmetic: 12.5 us -> none  [the longest x1 11 us: split_layer(): total = jnp.sum(weights, axis=-1, keepdims=True)]
  transfers between devices with their start and end apart: 17 -> 9, of which waited for: 14 -> 6; matrix products, arithmetic and copies ran while one was open for 25% -> 22% of each run, Pallas kernels for 0% -> 0%
where the time goes in v2:
time: 713 us; the launch traced here: 703 us
  waiting for transfers between devices  243 us (34%)
  Pallas kernels  158 us (22%)
  matrix products  115 us (16%)
  blocking collectives  73.3 us (10%)
  local copies, waits for them, and re-layouts  59.4 us (8%)
  other arithmetic  35.4 us (5%)
  between operations  15 us (2%)
    reduce_scatter x4, waiting for transfers between devices, scattered(): lax.psum_scatter(grad.astype(bf16), 'rows', scatter_dimension=0, tiled=True)  199 us
    pallas_call x1, Pallas kernels, forward(): pl.pallas_call(forward_kernel, out_shape=[jax.ShapeDtypeStruct(shape, kin...  158 us
    psum x1, blocking collectives, split_layer(): lax.psum((d_first_gain, d_first_shift, d_second_gain, d_second_shift, d_b...  41.2 us
    all_gather x3, blocking collectives, both(): return lax.all_gather(part, 'blk', axis=0).astype(f32)  32.1 us
    reduce_scatter x1, waiting for transfers between devices, split_layer(): lax.psum_scatter(down_part, 'blk', scatter_dimension=0, tiled=True)  31.4 us
    dot_general x1, matrix products, split_layer(): d_probs = jnp.einsum('hqe,hke->hqk', d_att3, v, preferred_element_type=f32)  19.7 us
    convert_element_type x1, other arithmetic, split_layer(): d_scores = (probs * (d_probs - row_dots)).astype(bf16)  16.3 us
  transfers between devices with their start and end apart: 9, of which 6 were waited for; matrix products, arithmetic and copies ran while one was open for 22% of the time, Pallas kernels for 0%

profile of v2, /device:TPU:0, one launch (start us, length us, event | category | flops | bytes accessed | tf_op | source)
XLA Modules:
  0.0 703.0 jit_solution(11428663148121941228)
XLA Ops:
  25.3 158.3 %forward.1 = (bf16[16,80,1920]{2,1,0:T(8,128)(2,1)}, bf16[16,80,1280]{2,1,0:T(8,128)(2,1)}, bf16[16,80,2560]{2,1,0:T(8,128)(2,1)}, bf16[16,160,1280]{2,1,0:T(8,1...) custom-call(bf16[384,1280]{1,0:T(8,128)(2,1)} %bitcast.92, ...), custom_call_target="tpu_custom_call" | custom-call | tf_op jit(solution)/shard_map/forward/pallas_call | solution.py:647
  183.6 9.7 %convert_reduce_fusion = (f32[2560]{0:T(1024)S(1)}, bf16[768,2560]{1,0:T(8,128)(2,1)S(1)}) fusion(bf16[768,2560]{1,0:T(8,128)(2,1)} %get-tuple-element.29, bf16[768,1280]{1,0:T(8,128)(2,1)} %bitcast.118, bf16[2560,1280]{1,0:T(8,128)(2,1)} %bitcast.113), kind=kOutput, calls=%fused_computation.8 | convolution fusion | flops 5042992640 | bytes 16394240 | tf_op jit(solution)/shard_map/tc,fc->tf/dot_general | solution.py:719
  195.2 6.4 convolution_convert_fusion.4
  201.7 10.2 %convolution_convert_fusion.5 = bf16[768,1280]{1,0:T(8,128)(2,1)} fusion(bf16[768,2560]{1,0:T(8,128)(2,1)} %get-tuple-element.26, bf16[2560,1280]{1,0:T(8,128)(2,1)} %bitcast.114), kind=kOutput, calls=%fused_computation.14 | convolution fusion | flops 5034147840 | bytes 12451840 | tf_op jit(solution)/shard_map/dot_general | solution.py:713
  212.0 4.8 copy.75
  221.6 9.6 %fusion.26 = f32[10,768,768]{1,2,0:T(8,128)} fusion(bf16[10,768,64]{1,2,0:T(8,128)(2,1)S(1)} %bitcast.95, bf16[10,768,64]{1,2,0:T(8,128)(2,1)S(1)} %bitcast.93), kind=kOutput, calls=%fused_computation.71 | convolution fusion | flops 754974720 | bytes 25559040 | tf_op jit(solution)/shard_map/hqe,hke->hqk/dot_general | solution.py:734
  236.8 31.4 %reduce-scatter.8.cloned.1.call-done = bf16[384,1280]{1,0:T(8,128)(2,1)} async-done(((bf16[768,1280]{1,0:T(8,128)(2,1)}), bf16[384,1280]{1,0:T(8,128)(2,1)}) %reduce-scatter.8.cloned.1.call-update) | async-done | bytes 983056 | tf_op jit(solution)/shard_map/reduce_scatter | solution.py:714
  281.0 4.7 convolution_convert_fusion.2
  285.8 7.9 %all-to-all-done = bf16[384,2,640]{2,0,1:T(8,128)(2,1)S(1)} async-done(((bf16[384,2,640]{2,0,1:T(8,128)(2,1)}), bf16[384,2,640]{2,0,1:T(8,128)(2,1)S(1)}, u32[]{:S(2)}, u32[]{:S(2)}) %all-to-all-start) | async-done | bytes 983072 | tf_op jit(solution)/shard_map/all_to_all | solution.py:732
  299.3 19.7 %multiply_reduce_fusion = (f32[10,768]{1,0:T(8,128)S(1)}, f32[10,768,768]{1,2,0:T(8,128)}) fusion(f32[10,768,768]{1,2,0:T(8,128)} %fusion.26, f32[10,768]{1,0:T(8,128)S(1)} %bitcast.109, pred[768,768]{0,1:T(8,128)(4,1)S(1)} %broadcast_compare_fusion, bf16[10,768,64]{1,2,0:T(8,128)(2,1)S(1)} %bitcast.102, bf16[768,10,64]{0,2,1:T(8,128)(2,1)S(1)} %reshape.231), kind=kOutput, calls=%fused_computation.1 | convolution fusion | flops 778560000 | bytes 49803264 | tf_op jit(solution)/shard_map/hqe,hke->hqk/dot_general | solution.py:736
  319.0 16.3 %multiply_convert_fusion = bf16[10,768,768]{1,2,0:T(8,128)(2,1)S(1)} fusion(f32[10,768,768]{1,2,0:T(8,128)} %get-tuple-element.61, f32[10,768,768]{1,2,0:T(8,128)} %fusion.26, f32[10,768]{1,0:T(8,128)S(1)} %get-tuple-element.60, f32[10,768]{1,0:T(8,128)S(1)} %bitcast.110, pred[768,768]{0,1:T(8,128)(4,1)S(1)} %broadcast_compare_fusion), kind=kLoop, calls=%fused_computation | loop fusion | flops 29491200 | bytes 59633664 | tf_op jit(solution)/shard_map/convert_element_type | solution.py:738
  342.1 11.0 %fusion.1 = bf16[10,64,768]{2,1,0:T(8,128)(2,1)} fusion(f32[10,768,768]{1,2,0:T(8,128)} %fusion.26, f32[10,768]{1,0:T(8,128)S(1)} %bitcast.111, pred[768,768]{0,1:T(8,128)(4,1)S(1)} %broadcast_compare_fusion, bf16[768,10,64]{0,2,1:T(8,128)(2,1)S(1)} %reshape.231), kind=kOutput, calls=%fused_computation.4 | convolution fusion | flops 772669440 | bytes 26179584 | tf_op jit(solution)/shard_map/hqk,hqe->khe/dot_general | solution.py:741
  356.5 8.2 %convolution_convert_fusion.6 = bf16[768,1280]{1,0:T(8,128)(2,1)} fusion(bf16[768,1920]{0,1:T(8,128)(2,1)S(1)} %bitcast.105, bf16[1280,1920]{1,0:T(8,128)(2,1)} %bitcast.116), kind=kOutput, calls=%fused_computation.15 | convolution fusion | flops 3775856640 | bytes 9830400 | tf_op jit(solution)/shard_map/tn,cn->tc/dot_general | solution.py:745
  365.4 10.3 %convolution_convert_fusion = bf16[2560,1280]{1,0:T(8,128)(2,1)} fusion(bf16[2560,768]{1,0:T(8,128)(2,1)} %get-tuple-element.38, bf16[768,1280]{1,0:T(8,128)(2,1)S(1)} %bitcast.119), kind=kOutput, calls=%fused_computation.6 | convolution fusion | flops 5036441600 | bytes 12451840 | tf_op jit(solution)/shard_map/dot_general | solution.py:718
  377.3 9.3 %convolution_convert_fusion.1 = bf16[1280,2560]{1,0:T(8,128)(2,1)} fusion(bf16[1280,768]{1,0:T(8,128)(2,1)S(1)} %copy-done.22, bf16[768,2560]{1,0:T(8,128)(2,1)} %copy-done.24), kind=kOutput, calls=%fused_computation.7 | convolution fusion | flops 5036441600 | bytes 12451840 | tf_op jit(solution)/shard_map/dot_general | solution.py:721
  388.1 7.7 %convolution_convert_fusion.3 = bf16[1280,1920]{1,0:T(8,128)(2,1)} fusion(bf16[1280,768]{1,0:T(8,128)(2,1)S(1)} %copy-done.21, bf16[768,1920]{0,1:T(8,128)(2,1)} %bitcast.106), kind=kOutput, calls=%fused_computation.11 | convolution fusion | flops 3777331200 | bytes 9830400 | tf_op jit(solution)/shard_map/dot_general | solution.py:744
  400.4 41.2 %all-reduce = (f32[1280]{0:T(1024)}, f32[1280]{0:T(1024)}, f32[1280]{0:T(1024)}, f32[1280]{0:T(1024)}, f32[5120]{0:T(1024)}) all-reduce(f32[1280]{0:T(1024)S(1)} %get-tuple-element.41, f32[1280]{0:T(1024)S(1)} %get-tuple-element.45, f32[1280]{0:T(1024)S(1)} %get-tuple-element.39, ...), channel_id=1, replica_groups=mesh['rows'=16,'blk'=2] {'rows','blk'}, use_global_device_ids=true, to_apply=%region_19.20 | all-reduce | flops 10240 | bytes 81920 | tf_op jit(solution)/shard_map/psum | solution.py:768
  447.5 63.9 %reduce-scatter.20.cloned.1.call-done = bf16[160,1280]{1,0:T(8,128)(2,1)} async-done(((bf16[2560,1280]{1,0:T(8,128)(2,1)}), bf16[160,1280]{1,0:T(8,128)(2,1)}) %reduce-scatter.20.cloned.1.call-update) | async-done | bytes 409616 | tf_op jit(solution)/shard_map/reduce_scatter | solution.py:754
  511.4 11.6 %all-gather.2 = bf16[320,1280]{1,0:T(8,128)(2,1)S(1)} all-gather(bf16[160,1280]{1,0:T(8,128)(2,1)} %reduce-scatter.20.cloned.1.call-done), channel_id=4, replica_groups=mesh['rows'=16,'blk'=2] {'blk'}, dimensions={0}, use_global_device_ids=true | all-gather | bytes 1228800 | tf_op jit(solution)/shard_map/all_gather | solution.py:757
  524.3 77.6 %reduce-scatter.18.cloned.1.call-done = bf16[80,2560]{1,0:T(8,128)(2,1)} async-done(((bf16[1280,2560]{1,0:T(8,128)(2,1)}), bf16[80,2560]{1,0:T(8,128)(2,1)}) %reduce-scatter.18.cloned.1.call-update) | async-done | bytes 409616 | tf_op jit(solution)/shard_map/reduce_scatter | solution.py:754
  601.9 11.6 %all-gather.1 = bf16[160,2560]{1,0:T(8,128)(2,1)S(1)} all-gather(bf16[80,2560]{1,0:T(8,128)(2,1)} %reduce-scatter.18.cloned.1.call-done), channel_id=3, replica_groups=mesh['rows'=16,'blk'=2] {'blk'}, dimensions={0}, use_global_device_ids=true | all-gather | bytes 1228800 | tf_op jit(solution)/shard_map/all_gather | solution.py:757
  619.0 5.9 reshape.245
  624.9 57.4 %reduce-scatter.14.cloned.1.call-done = bf16[80,1920]{1,0:T(8,128)(2,1)} async-done(((bf16[1280,1920]{1,0:T(8,128)(2,1)}), bf16[80,1920]{1,0:T(8,128)(2,1)}) %reduce-scatter.14.cloned.1.call-update) | async-done | bytes 307216 | tf_op jit(solution)/shard_map/reduce_scatter | solution.py:754
  682.3 8.9 %all-gather = bf16[160,1920]{1,0:T(8,128)(2,1)S(1)} all-gather(bf16[80,1920]{1,0:T(8,128)(2,1)} %reduce-scatter.14.cloned.1.call-done), channel_id=2, replica_groups=mesh['rows'=16,'blk'=2] {'blk'}, dimensions={0}, use_global_device_ids=true | all-gather | bytes 921600 | tf_op jit(solution)/shard_map/all_gather | solution.py:757
  (124 shorter events, 84.3 us)
Async XLA Ops:
  7.2 17.3 %copy-start = (bf16[320,1280]{1,0:T(8,128)(2,1)S(1)}, bf16[320,1280]{1,0:T(8,128)(2,1)}, u32[]{:S(2)}) copy-start(bf16[320,1280]{1,0:T(8,128)(2,1)} %param.22) | copy-start | bytes 2457604
  7.2 10.0 %copy-start.14 = (bf16[80,5120]{1,0:T(8,128)(2,1)S(1)}, bf16[80,5120]{1,0:T(8,128)(2,1)}, u32[]{:S(2)}) copy-start(bf16[80,5120]{1,0:T(8,128)(2,1)} %param.20) | copy-start | bytes 2457604
  7.2 227.7 %reduce-scatter.10.cloned.1.call-start = ((), (), s32[]{:S(2)}) async-start(), calls=%async_computation.9 | async-start | bytes 2949120 | tf_op jit(solution)/shard_map/reduce_scatter | solution.py:723
  183.6 11.6 %copy-start.19 = (bf16[16,80,2560]{2,1,0:T(8,128)(2,1)S(1)}, bf16[16,80,2560]{2,1,0:T(8,128)(2,1)}, u32[]{:S(2)}) copy-start(bf16[16,80,2560]{2,1,0:T(8,128)(2,1)} %get-tuple-element.30) | copy-start | bytes 19660804
  201.7 66.6 %reduce-scatter.8.cloned.1.call-start = ((), (), s32[]{:S(2)}) async-start(), calls=%async_computation.8 | async-start | bytes 2949120 | tf_op jit(solution)/shard_map/reduce_scatter | solution.py:714
  212.0 4.8 copy-start.2
  212.0 4.9 copy-start.18
  221.6 13.3 %copy-start.17 = (f32[1280]{0:T(1024)S(1)}, f32[1280]{0:T(1024)}, u32[]{:S(2)}) copy-start(f32[1280]{0:T(1024)} %param.18) | copy-start | bytes 15364
  268.2 3.6 copy-start.9
  271.8 4.1 copy-start.4
  276.9 16.7 %all-to-all-start = ((bf16[384,2,640]{2,0,1:T(8,128)(2,1)}), bf16[384,2,640]{2,0,1:T(8,128)(2,1)S(1)}, u32[]{:S(2)}, u32[]{:S(2)}) async-start(bf16[384,2,640]{2,0,1:T(8,128)(2,1)} %bitcast.90), calls=%async_computation.2 | async-start | bytes 1966080 | tf_op jit(solution)/shard_map/all_to_all | solution.py:732
  280.5 84.3 %reduce-scatter.16.cloned.1.call-start = ((), (), s32[]{:S(2)}) async-start(), calls=%async_computation.12 | async-start | bytes 3481600 | tf_op jit(solution)/shard_map/reduce_scatter | solution.py:754
  285.7 13.5 %copy-start.12 = (bf16[768,5,1,2,64]{0,4,3,2,1:T(8,128)(2,1)S(1)}, bf16[768,5,1,2,64]{0,4,3,2,1:T(8,128)(2,1)}, u32[]{:S(2)}) copy-start(bf16[768,5,1,2,64]{0,4,3,2,1:T(8,128)(2,1)} %get-tuple-element.54) | copy-start | bytes 2949124
  285.7 13.5 %copy-start.15 = (f32[16,768]{1,0:T(8,128)S(1)}, f32[16,768]{1,0:T(8,128)}, u32[]{:S(2)}) copy-start(f32[16,768]{1,0:T(8,128)} %get-tuple-element.32) | copy-start | bytes 147460
  285.7 111.5 %reduce-scatter.12.cloned.1.call-start = ((), (), s32[]{:S(2)}) async-start(), calls=%async_computation.10 | async-start | bytes 2949120 | tf_op jit(solution)/shard_map/reduce_scatter | solution.py:746
  319.0 16.3 %copy-start.8 = (bf16[768,5,1,2,64]{0,4,3,2,1:T(8,128)(2,1)S(1)}, bf16[768,5,1,2,64]{0,4,3,2,1:T(8,128)(2,1)}, u32[]{:S(2)}) copy-start(bf16[768,5,1,2,64]{0,4,3,2,1:T(8,128)(2,1)} %copy-done.7) | copy-start | bytes 2949124
  335.3 4.6 copy-start.6
  356.5 8.9 %copy-start.23 = (bf16[2,384,1280]{2,1,0:T(8,128)(2,1)S(1)}, bf16[2,384,1280]{2,1,0:T(8,128)(2,1)}, u32[]{:S(2)}) copy-start(bf16[2,384,1280]{2,1,0:T(8,128)(2,1)} %get-tuple-element.28) | copy-start | bytes 5898244
  364.8 81.0 %all-reduce.3.cloned.1.call-start = ((), (), s32[]{:S(2)}) async-start(), calls=%async_computation.13 | async-start | bytes 409600 | tf_op jit(solution)/shard_map/psum | solution.py:764
  365.4 146.1 %reduce-scatter.20.cloned.1.call-start = ((), (), s32[]{:S(2)}) async-start(), calls=%async_computation.15 | async-start | bytes 6963200 | tf_op jit(solution)/shard_map/reduce_scatter | solution.py:754
  375.8 226.1 %reduce-scatter.18.cloned.1.call-start = ((), (), s32[]{:S(2)}) async-start(), calls=%async_computation.14 | async-start | bytes 6963200 | tf_op jit(solution)/shard_map/reduce_scatter | solution.py:754
  386.6 295.7 %reduce-scatter.14.cloned.1.call-start = ((), (), s32[]{:S(2)}) async-start(), calls=%async_computation.11 | async-start | bytes 5222400 | tf_op jit(solution)/shard_map/reduce_scatter | solution.py:754
  397.0 44.5 %copy-start.10 = (bf16[1,384,1280]{2,1,0:T(8,128)(2,1)S(1)}, bf16[1,384,1280]{2,1,0:T(8,128)(2,1)}, u32[]{:S(2)}) copy-start(bf16[1,384,1280]{2,1,0:T(8,128)(2,1)} %param.23) | copy-start | bytes 2949124
  692.6 3.1 copy-start.1
  (10 other events, 16.2 us)
Sparse Core Ops, SparseCore 0:
  201.8 33.0 reduce-scatter.9
  237.8 30.3 reduce-scatter.7
  285.8 68.2 reduce-scatter.15
  364.9 30.4 reduce-scatter.11
  397.5 22.9 all-reduce.2
  424.4 87.0 reduce-scatter.19
  515.9 85.9 reduce-scatter.17
  605.9 76.3 reduce-scatter.13
